TPU v7x, 256 devices: a whole 4x4x8 slice. The times are simulated.
256 devices in a mesh: dp: 32 (over x, z), tensor: 8 (over y, core).
Axes of the slice: x: 4, y: 4, z: 8, core: 2. Of those that a mesh axis runs over, the one named last changes fastest.
Arguments:
- patches: bfloat16 [32768, 1176], P('dp')
- rank_groups: int32 [32], P('dp'), may hold values from 1 to 256, 4096 in all
- patch_weight: bfloat16 [1176, 1280], P(None, 'tensor')
- merge_weight: bfloat16 [4, 1280, 8192], P(None, 'tensor', 'dp'), may hold values from -0.078125 to 0.078125
- emb_grad: bfloat16 [8192, 8192], P('dp', 'tensor'), may hold values from -6 to 6
Outputs:
- embeds: bfloat16 [8192, 8192], P('dp', 'tensor')
- grad_merge: float32 [4, 1280, 8192], P(None, 'tensor', 'dp')
- grad_patch: float32 [1176, 1280], P(None, 'tensor')
Inputs may be any that keep to these rules, and one draw needn't show every extreme that they name: `rank_groups`: the counts of all dp ranks add up to 4096; some rank holds exactly 256.
All inputs are finite; a program needn't handle non-finite values. No bound on the sum of `rank_groups` on one device may be relied on, other than what follows from the above.
Results may differ from a plain program's by a relative error of at most 0.02.
Values may be sent and summed in bfloat16 or wider, within the bound.
A program may use at most 128 MiB of HBM per device.

v0:
```python
import jax
import jax.numpy as jnp
from jax import lax
from jax.sharding import PartitionSpec as P

E = 1280


def encode_forward(enc_rows, patch_weight, whole_merge):
    projected = jnp.dot(enc_rows, patch_weight, preferred_element_type=jnp.float32)
    row_sums = jnp.sum(projected, axis=1)
    square_sums = jnp.sum(projected * projected, axis=1)
    total_sums, total_squares = lax.psum((row_sums, square_sums), "tensor")
    row_mean = total_sums[:, None] / E
    square = total_squares[:, None] / E
    inv_scale = lax.rsqrt(square - row_mean * row_mean + 1e-05)
    normed = (projected - row_mean) * inv_scale
    feat_share = patch_weight.shape[1]
    merged = normed.reshape(enc_rows.shape[0] // 4, 4 * feat_share).astype(jnp.bfloat16)
    merge_table = whole_merge.reshape(4 * feat_share, whole_merge.shape[2])
    partial_terms = jnp.dot(merged, merge_table, preferred_element_type=jnp.float32)
    embed_share = lax.psum_scatter(
        partial_terms.astype(jnp.bfloat16), "tensor", scatter_dimension=1, tiled=True
    ).astype(jnp.float32)
    return (embed_share, merged, normed, inv_scale, merge_table)


def merge_gradient(merged, cot_full, feat_share):
    d_total = cot_full.shape[1]
    merge_term = lax.dot_general(
        merged, cot_full, (((0,), (0,)), ((), ())), preferred_element_type=jnp.float32
    )
    return lax.psum_scatter(
        merge_term.reshape(4, feat_share, d_total).astype(jnp.bfloat16),
        "dp",
        scatter_dimension=2,
        tiled=True,
    ).astype(jnp.float32)


def home_backward(merged, cot_share, merge_table, feat_share):
    cot_full = lax.all_gather(cot_share, "tensor", axis=1, tiled=True)
    dmerged = lax.dot_general(
        cot_full, merge_table, (((1,), (1,)), ((), ())), preferred_element_type=jnp.float32
    )
    grad_merge = merge_gradient(merged, cot_full, feat_share)
    return (dmerged, grad_merge)


def norm_backward(enc_rows, dnormed, normed, inv_scale):
    first_sums = jnp.sum(dnormed, axis=1)
    second_sums = jnp.sum(dnormed * normed, axis=1)
    first_total, second_total = lax.psum((first_sums, second_sums), "tensor")
    grad_input = (
        (dnormed - first_total[:, None] / E - normed * (second_total[:, None] / E)) * inv_scale
    ).astype(jnp.bfloat16)
    patch_term = lax.dot_general(
        enc_rows, grad_input, (((0,), (0,)), ((), ())), preferred_element_type=jnp.float32
    )
    return lax.psum(patch_term.astype(jnp.bfloat16), "dp").astype(jnp.float32)


def body(patches, rank_groups, patch_weight, merge_weight, emb_grad):
    whole_merge = lax.all_gather(merge_weight, "dp", axis=2, tiled=True)
    feat_share = patch_weight.shape[1]
    slot_count = emb_grad.shape[0]
    live_count = rank_groups[0]
    position = jnp.arange(slot_count, dtype=jnp.int32)
    live_mask = (position < live_count)[:, None]
    cot_share = jnp.where(live_mask, emb_grad, jnp.zeros_like(emb_grad))
    embed_share, merged, normed, inv_scale, merge_table = encode_forward(
        patches, patch_weight, whole_merge
    )
    rounded = embed_share.astype(jnp.bfloat16)
    embeds = jnp.where(live_mask, rounded, jnp.zeros_like(rounded))
    dmerged, grad_merge = home_backward(merged, cot_share, merge_table, feat_share)
    dnormed = dmerged.reshape(normed.shape)
    grad_patch = norm_backward(patches, dnormed, normed, inv_scale)
    return (embeds, grad_merge, grad_patch)


def solution(mesh):
    return jax.shard_map(
        body,
        mesh=mesh,
        in_specs=(
            P("dp", None),
            P("dp"),
            P(None, "tensor"),
            P(None, "tensor", "dp"),
            P("dp", "tensor"),
        ),
        out_specs=(P("dp", "tensor"), P(None, "tensor", "dp"), P(None, "tensor")),
        check_vma=False,
    )
```

profile of v0, /device:TPU:1, one launch (start us, length us, event | category | flops | bytes accessed | tf_op | source)
XLA Modules:
  0.0 619.0 jit_solution(5486657557005063351)
XLA Ops:
  7.2 0.0 copy-start
  7.2 0.0 all-gather.5.cloned.1.call-start
  8.0 1.9 broadcast_select_fusion
  10.0 0.0 all-gather.5.cloned.1.call-update
  10.0 0.0 all-gather.3.cloned.1.call-start
  10.1 0.7 all-gather.3.cloned.1.call-update
  10.8 0.0 all-reduce.4.cloned.1.call-start
  10.8 0.0 copy-done
  10.8 2.4 fusion.7
  13.2 15.2 %all-reduce.1 = (f32[1024]{0:T(1024)S(1)}, f32[1024]{0:T(1024)S(1)}) all-reduce(f32[1024]{0:T(1024)S(1)} %get-tuple-element.4, f32[1024]{0:T(1024)S(1)} %get-tuple-element.3), channel_id=1, replica_groups=mesh['dp'=32,'tensor'=8] {'tensor'}, use_global_device_ids=true, to_apply=%region_3.4 | all-reduce | flops 2048 | bytes 16384 | tf_op jit(solution)/shard_map/psum | solution.py:13
  28.5 20.9 %all-gather.5.cloned.1.call-done = bf16[256,8192]{1,0:T(8,128)(2,1)} async-done(((bf16[256,1024]{1,0:T(8,128)(2,1)}), bf16[256,8192]{1,0:T(8,128)(2,1)}) %all-gather.5.cloned.1.call-update) | async-done | bytes 4194320 | tf_op jit(solution)/shard_map/all_gather | solution.py:42
  49.4 114.8 %all-gather.3.cloned.1.call-done = bf16[4,160,8192]{2,1,0:T(8,128)(2,1)} async-done(((bf16[4,160,256]{2,1,0:T(8,128)(2,1)}), bf16[4,160,8192]{2,1,0:T(8,128)(2,1)}) %all-gather.3.cloned.1.call-update) | async-done | bytes 10485776 | tf_op jit(solution)/shard_map/all_gather | solution.py:64
  164.2 9.5 %fusion.8 = f32[256,640]{1,0:T(8,128)} fusion(bf16[256,8192]{1,0:T(8,128)(2,1)} %all-gather.5.cloned.1.call-done, bf16[640,8192]{1,0:T(8,128)(2,1)} %bitcast.20), kind=kOutput, calls=%fused_computation.22 | convolution fusion | flops 2684354560 | bytes 15335424 | tf_op jit(solution)/shard_map/dot_general | solution.py:43
  173.7 1.5 reshape.34
  175.2 1.2 copy.14
  176.4 0.2 reduce_sum.38
  176.6 1.4 multiply_reduce_fusion
  178.0 15.1 %all-reduce = (f32[1024]{0:T(1024)S(1)}, f32[1024]{0:T(1024)S(1)}) all-reduce(f32[1024]{0:T(1024)S(1)} %get-tuple-element.9, f32[1024]{0:T(1024)S(1)} %reduce_sum.38), channel_id=1, replica_groups=mesh['dp'=32,'tensor'=8] {'tensor'}, use_global_device_ids=true, to_apply=%region_9.10 | all-reduce | flops 2048 | bytes 16384 | tf_op jit(solution)/shard_map/psum | solution.py:53
  193.2 3.0 fusion.1
  196.1 0.0 all-reduce.4.cloned.1.call-update
  196.2 0.0 reduce-scatter.3.cloned.1.call-start
  196.2 0.2 copy.12
  196.4 0.7 convert_element_type.31
  197.1 9.0 %convolution_convert_fusion.1 = bf16[256,8192]{1,0:T(8,128)(2,1)} fusion(bf16[256,640]{1,0:T(8,128)(2,1)S(1)} %convert_element_type.31, bf16[640,8192]{1,0:T(8,128)(2,1)} %bitcast.21), kind=kOutput, calls=%fused_computation.1 | convolution fusion | flops 2686451712 | bytes 15007744 | tf_op jit(solution)/shard_map/dot_general | solution.py:21
  206.1 0.0 reduce-scatter.3.cloned.1.call-update
  206.1 0.0 reduce-scatter.5.cloned.1.call-start
  206.1 0.2 copy.13
  206.3 7.8 %convolution_convert_fusion = bf16[4,160,8192]{2,1,0:T(8,128)(2,1)} fusion(bf16[4,160,256]{2,1,0:T(8,128)(2,1)S(1)} %bitcast.19, bf16[256,8192]{1,0:T(8,128)(2,1)} %all-gather.5.cloned.1.call-done), kind=kOutput, calls=%fused_computation | convolution fusion | flops 2689597440 | bytes 15007744 | tf_op jit(solution)/shard_map/dot_general | solution.py:30
  214.1 0.0 reduce-scatter.5.cloned.1.call-update
  214.1 118.8 %all-reduce.4.cloned.1.call-done = bf16[1176,160]{0,1:T(8,128)(2,1)} async-done(((bf16[1176,160]{0,1:T(8,128)(2,1)}), bf16[1176,160]{0,1:T(8,128)(2,1)}) %all-reduce.4.cloned.1.call-update) | async-done | bytes 376336 | tf_op jit(solution)/shard_map/psum | solution.py:60
  332.9 1.9 convert_element_type.38
  334.9 40.1 %reduce-scatter.3.cloned.1.call-done = bf16[256,1024]{1,0:T(8,128)(2,1)} async-done(((bf16[256,8192]{1,0:T(8,128)(2,1)}), bf16[256,1024]{1,0:T(8,128)(2,1)}) %reduce-scatter.3.cloned.1.call-update) | async-done | bytes 524304 | tf_op jit(solution)/shard_map/reduce_scatter | solution.py:22
  374.9 1.9 broadcast_select_fusion.1
  376.9 233.7 %reduce-scatter.5.cloned.1.call-done = bf16[4,160,256]{2,1,0:T(8,128)(2,1)} async-done(((bf16[4,160,8192]{2,1,0:T(8,128)(2,1)}), bf16[4,160,256]{2,1,0:T(8,128)(2,1)}) %reduce-scatter.5.cloned.1.call-update) | async-done | bytes 327696 | tf_op jit(solution)/shard_map/reduce_scatter | solution.py:33
  610.6 1.9 convert_element_type.34
  (3 shorter events, 0.0 us)
Async XLA Ops:
  7.2 3.6 copy-start
  7.2 42.2 %all-gather.5.cloned.1.call-start = ((), (), s32[]{:S(2)}) async-start(), calls=%async_computation.4 | async-start | bytes 4718592 | tf_op jit(solution)/shard_map/all_gather | solution.py:42
  10.0 154.2 %all-gather.3.cloned.1.call-start = ((), (), s32[]{:S(2)}) async-start(), calls=%async_computation.2 | async-start | bytes 10813440 | tf_op jit(solution)/shard_map/all_gather | solution.py:64
  10.8 322.2 %all-reduce.4.cloned.1.call-start = ((), (), s32[]{:S(2)}) async-start(), calls=%async_computation.6 | async-start | bytes 819200 | tf_op jit(solution)/shard_map/psum | solution.py:60
  196.2 178.8 %reduce-scatter.3.cloned.1.call-start = ((), (), s32[]{:S(2)}) async-start(), calls=%async_computation.3 | async-start | bytes 4718592 | tf_op jit(solution)/shard_map/reduce_scatter | solution.py:22
  206.1 404.5 %reduce-scatter.5.cloned.1.call-start = ((), (), s32[]{:S(2)}) async-start(), calls=%async_computation.5 | async-start | bytes 10813440 | tf_op jit(solution)/shard_map/reduce_scatter | solution.py:33
Sparse Core Ops, SparseCore 0:
  10.4 38.8 all-gather.4
  51.8 112.3 all-gather.2
  196.3 136.5 all-reduce.3
  335.5 39.4 reduce-scatter.2
  379.4 231.1 reduce-scatter.4
where the time goes:
time: 623 us; the launch traced here: 619 us
  waiting for transfers between devices  529 us (85%)
  matrix products  31.7 us (5%)
  blocking collectives  30.3 us (5%)
  between operations  14.7 us (2%)
  other arithmetic  9.34 us (1%)
    reduce_scatter x1, waiting for transfers between devices, merge_gradient(): lax.psum_scatter(merge_term.reshape(4, feat_share, d_total).astype(jnp.bf...  234 us
    psum x1, waiting for transfers between devices, norm_backward(): return lax.psum(patch_term.astype(jnp.bfloat16), 'dp').astype(jnp.float32)  119 us
    all_gather x1, waiting for transfers between devices, body(): whole_merge = lax.all_gather(merge_weight, 'dp', axis=2, tiled=True)  115 us
    reduce_scatter x1, waiting for transfers between devices, encode_forward(): lax.psum_scatter(partial_terms.astype(jnp.bfloat16), 'tensor', scatter_di...  40.1 us
    all_gather x1, waiting for transfers between devices, home_backward(): cot_full = lax.all_gather(cot_share, 'tensor', axis=1, tiled=True)  20.9 us
    psum x1, blocking collectives, encode_forward(): total_sums, total_squares = lax.psum((row_sums, square_sums), 'tensor')  15.2 us
    psum x1, blocking collectives, norm_backward(): first_total, second_total = lax.psum((first_sums, second_sums), 'tensor')  15.1 us
  transfers between devices with their start and end apart: 5, of which 5 were waited for; matrix products, arithmetic and copies ran while one was open for 4% of the time, Pallas kernels for 0%

commit v1 on v0

v1 whole, which is shorter than its diff:
```python
import functools

import jax
import jax.numpy as jnp
from jax import lax
from jax.experimental import pallas as pl
from jax.experimental.pallas import tpu as pltpu
from jax.sharding import PartitionSpec as P

E = 1280
X, Y, Z = 4, 4, 8
T = 2 * Y
F32, BF16 = jnp.float32, jnp.bfloat16
HIGH = lax.Precision.HIGHEST

PD = 1176
FS = E // T
K = 4 * FS
G = 256
NC = 256
HALF = K // 2
QUAD = Z // 2


def dot(a, b, dims=((1,), (0,)), precision=None):
    return lax.dot_general(a, b, (dims, ((), ())), precision=precision, preferred_element_type=F32)


def wrap(value, count):
    return lax.rem(value + count, count)


def group_rows(offset):
    row = lax.broadcasted_iota(jnp.int32, (8, K), 0)
    lane = lax.broadcasted_iota(jnp.int32, (8, K), 1)
    low = (row - offset) * FS
    return jnp.where((lane >= low) & (lane < low + FS), 1.0, 0.0).astype(F32)


def kernel(
    live_ref, patches_ref, pw_ref, w_ref, emb_ref,
    embeds_ref, gm_ref, gp_ref,
    wg, cot_own, cot_y, cot_all, merged_all, merged_t, proj_s, pw_s, normed_s,
    stats, g_send_buf, g_recv_buf, d_send_buf, d_own, d_recv_buf,
    e_sib_send, e_sib_recv, e_send, e_recv, e_sum, e_fin,
    t_s, a_own, a_xr, a_x, a_zr, a_all,
    w_ss, w_rs, tr_ss, tr_rs, cy_ss, cy_rs, cs_ss, cs_rs, st_ss, st_rs, m_ss, m_rs,
    d_ss, d_rs, g_ss, g_rs, es_ss, es_rs, ey_ss, ey_rs, ax_ss, ax_rs, az_ss, az_rs,
    bz_ss, bz_rs, bx_ss, bx_rs,
):
    dp = lax.axis_index("dp")
    t = lax.axis_index("tensor")
    x, z = lax.div(dp, Z), lax.rem(dp, Z)
    y, c = lax.div(t, 2), lax.rem(t, 2)

    def device(x, y, z, c):
        return (x * Z + z, y * 2 + c)

    started = []

    def send(src, dst, ssem, rsem, to):
        copy = pltpu.make_async_remote_copy(
            src_ref=src, dst_ref=dst, send_sem=ssem, recv_sem=rsem,
            device_id=to, device_id_type=pl.DeviceIdType.MESH,
        )
        copy.start()
        started.append(copy)

    def arrived(dst, rsem, to):
        pltpu.make_async_remote_copy(
            src_ref=dst, dst_ref=dst, send_sem=w_ss.at[0, 0, 0], recv_sem=rsem,
            device_id=to, device_id_type=pl.DeviceIdType.MESH,
        ).wait_recv()

    right = device(x, y, wrap(z + 1, Z), c)
    left = device(x, y, wrap(z - 1, Z), c)
    sibling = device(x, y, z, 1 - c)
    partner = device(y, x, z, c)
    x_peers = [device(wrap(x + k, X), y, z, c) for k in range(1, X)]
    y_peers = [device(x, wrap(y + k, Y), z, c) for k in range(1, Y)]
    z_peers = [device(x, y, wrap(z + k, Z), c) for k in range(1, Z)]
    t_peers = [(dp, wrap(t + k, T)) for k in range(1, T)]
    diagonal = x == y

    barrier = pltpu.get_barrier_semaphore()
    greeted = x_peers + z_peers + t_peers
    for peer in greeted:
        pl.semaphore_signal(barrier, inc=1, device_id=peer, device_id_type=pl.DeviceIdType.MESH)

    @pl.when(jnp.logical_not(diagonal))
    def _():
        pl.semaphore_signal(barrier, inc=1, device_id=partner, device_id_type=pl.DeviceIdType.MESH)

    pl.semaphore_wait(barrier, len(greeted) + jnp.where(diagonal, 0, 1))

    wg[z] = w_ref[...]

    def w_part(index, half):
        return wg.at[index, pl.ds(half * HALF, HALF)]

    def w_halves(way, step):
        return (0, 1) if step < 3 else (way,)

    def w_send(step):
        for way, to, block in ((0, right, wrap(z - step, Z)), (1, left, wrap(z + step, Z))):
            for half in w_halves(way, step):
                if step:
                    arrived(w_part(block, half), w_rs.at[way, step - 1, half], to)
                send(w_part(block, half), w_part(block, half), w_ss.at[way, step, half],
                     w_rs.at[way, step, half], to)

    def w_finish():
        for way, block in ((0, wrap(z - 3, Z)), (1, wrap(z + 3, Z))):
            half = 1 - way
            arrived(w_part(block, half), w_rs.at[way, 2, half], right)
        for way in (0, 1):
            arrived(w_part(wrap(z + 4, Z), way), w_rs.at[way, 3, way], right)

    w_send(0)

    live = live_ref[0]

    def live_rows(columns):
        return lax.broadcasted_iota(jnp.int32, (G, columns), 0) < live

    for k in range(QUAD):
        block = emb_ref[:, k * NC:(k + 1) * NC]
        cot_own[k] = jnp.where(live_rows(NC), block, jnp.zeros_like(block))

    def swap_start(src, dst, index):
        @pl.when(diagonal)
        def _():
            pltpu.make_async_copy(src, dst, tr_rs.at[index]).start()

        @pl.when(jnp.logical_not(diagonal))
        def _():
            pltpu.make_async_remote_copy(
                src_ref=src, dst_ref=dst, send_sem=tr_ss.at[index], recv_sem=tr_rs.at[index],
                device_id=partner, device_id_type=pl.DeviceIdType.MESH,
            ).start()

    def swap_wait(src, dst, index):
        @pl.when(diagonal)
        def _():
            pltpu.make_async_copy(src, dst, tr_rs.at[index]).wait()

        @pl.when(jnp.logical_not(diagonal))
        def _():
            pltpu.make_async_remote_copy(
                src_ref=src, dst_ref=dst, send_sem=tr_ss.at[index], recv_sem=tr_rs.at[index],
                device_id=partner, device_id_type=pl.DeviceIdType.MESH,
            ).wait()

    swap_start(cot_own, cot_y, 0)

    pw_s[...] = jnp.zeros_like(pw_s)
    pw_s[:, :FS] = pw_ref[...]

    @pl.loop(0, 4)
    def _(i):
        rows = pl.ds(i * 256, 256)
        product = dot(patches_ref[rows, :], pw_s[...])
        proj_s[0, rows] = product[:, :128]
        proj_s[1, rows] = product[:, 128:]

    parts = []
    for q in range(4):
        rows = pl.ds(q, G, stride=4)
        parts.append(jnp.concatenate([proj_s[0, rows, :], proj_s[1, rows, :]], axis=1)[:, :FS])
    projected = jnp.concatenate(parts, axis=1)

    first, second = group_rows(0), group_rows(4)

    def sums_over_tensor(index, one, two):
        stats[index, t] = (
            dot(first, one, ((1,), (1,)), HIGH) + dot(second, two, ((1,), (1,)), HIGH)
        )
        for k, peer in enumerate(t_peers):
            send(stats.at[index, t], stats.at[index, t], st_ss.at[index, k], st_rs.at[index, k], peer)

    def totals(index):
        for k, peer in enumerate(t_peers):
            owner = wrap(t - 1 - k, T)
            arrived(stats.at[index, owner], st_rs.at[index, k], peer)
        total = stats[index, 0]
        for k in range(1, T):
            total = total + stats[index, k]
        return total / E

    def spread(rows, value):
        return dot(value, rows, ((0,), (0,)), HIGH)

    sums_over_tensor(0, projected, projected * projected)

    def forward_cot():
        for k, peer in enumerate(y_peers):
            send(cot_y, cot_all.at[y, pl.ds(c * QUAD, QUAD)], cy_ss.at[k], cy_rs.at[k], peer)
        mine = cot_all.at[y, pl.ds(c * QUAD, QUAD)]
        send(cot_y, mine, cs_ss.at[0], cs_rs.at[0], sibling)
        mine[...] = cot_y[...]

    swap_wait(cot_own, cot_y, 0)
    forward_cot()

    means = totals(0)
    row = lax.broadcasted_iota(jnp.int32, (8, G), 0)
    row_mean = pltpu.roll(means, 4, 0)
    inv_scale = jnp.where(row >= 4, lax.rsqrt(
        jnp.where(row >= 4, means - row_mean * row_mean, 1.0) + 1e-05), 0.0)
    inv_wide = spread(second, inv_scale)
    normed = (projected - spread(first, means)) * inv_wide
    normed_s[0] = normed
    normed_s[1] = inv_wide
    merged_all[x] = normed.astype(BF16)
    for k, peer in enumerate(x_peers):
        send(merged_all.at[x], merged_all.at[x], m_ss.at[k], m_rs.at[k], peer)

    w_send(1)
    for k, peer in enumerate(y_peers):
        block = cot_all.at[wrap(y - 1 - k, Y), pl.ds(c * QUAD, QUAD)]
        arrived(block, cy_rs.at[k], peer)
        send(block, block, cs_ss.at[k + 1], cs_rs.at[k + 1], sibling)
    w_send(2)
    for k, peer in enumerate(x_peers):
        arrived(merged_all.at[wrap(x - 1 - k, X)], m_rs.at[k], peer)
    for i in range(X):
        merged_t[:, i * G:(i + 1) * G] = jnp.transpose(merged_all[i])
    for k in range(4):
        block = cot_all.at[wrap(y - k, Y), pl.ds((1 - c) * QUAD, QUAD)]
        arrived(block, cs_rs.at[k], sibling)

    def merge_term(block):
        return dot(merged_t[...], cot_all[:, block].reshape(X * G, NC))

    def g_send(step):
        for way, to, block in ((0, right, wrap(z + 4 - step, Z)), (1, left, wrap(z - 4 + step, Z))):
            term = merge_term(block)
            for half in (0, 1) if step else (way,):
                value = term[half * HALF:(half + 1) * HALF]
                if step > 1 or (step == 1 and half == way):
                    arrived(g_recv_buf.at[way, step - 1, half], g_rs.at[way, step - 1, half], to)
                    value = value + g_recv_buf[way, step - 1, half].astype(F32)
                g_send_buf[way, step, half] = value.astype(BF16)
                send(g_send_buf.at[way, step, half], g_recv_buf.at[way, step, half],
                     g_ss.at[way, step, half], g_rs.at[way, step, half], to)

    g_send(0)
    w_send(3)
    w_finish()

    def d_term(owner):
        total = None
        for block in range(Z):
            term = dot(cot_all[owner, block], wg[block], ((1,), (1,)))
            total = term if total is None else total + term
        return total

    @pl.loop(0, X - 1)
    def _(k):
        d_send_buf[k] = d_term(wrap(x + 1 + k, X)).astype(BF16)

    for k, peer in enumerate(x_peers):
        send(d_send_buf.at[k], d_recv_buf.at[k], d_ss.at[k], d_rs.at[k], peer)
    d_own[...] = d_term(x)

    g_send(1)

    @pl.loop(0, QUAD)
    def _(k):
        block = wg[(1 - c) * QUAD + k]
        for i in range(X):
            e_sib_send[k, i] = dot(merged_all[i], block).astype(BF16)

    for k in range(QUAD):
        send(e_sib_send.at[k], e_sib_recv.at[k], es_ss.at[k], es_rs.at[k], sibling)

    for k in range(X - 1):
        arrived(d_recv_buf.at[k], d_rs.at[k], sibling)
    dnormed = d_own[...]
    for k in range(X - 1):
        dnormed = dnormed + d_recv_buf[k].astype(F32)
    normed = normed_s[0]
    sums_over_tensor(1, dnormed, dnormed * normed)
    d_own[...] = dnormed

    for k in range(QUAD):
        arrived(e_sib_recv.at[k], es_rs.at[k], sibling)

    @pl.loop(0, QUAD)
    def _(k):
        block = wg[c * QUAD + k]
        for i in range(X):
            value = dot(merged_all[i], block) + e_sib_recv[k, i].astype(F32)
            e_send[i, k] = value.astype(BF16)

    for k, peer in enumerate(y_peers):
        send(e_send.at[wrap(y + 1 + k, Y)], e_recv.at[k], ey_ss.at[k], ey_rs.at[k], peer)

    means = totals(1)
    d_mean = spread(first, means)
    dn_mean = spread(second, means)
    grad_input = (d_own[...] - d_mean - normed_s[0] * dn_mean) * normed_s[1]
    for q in range(4):
        part = grad_input[:, q * FS:(q + 1) * FS]
        part = jnp.concatenate([part, jnp.zeros((G, 256 - FS), F32)], axis=1)
        rows = pl.ds(q, G, stride=4)
        proj_s[0, rows, :] = part[:, :128]
        proj_s[1, rows, :] = part[:, 128:]
    grad_rows = jnp.concatenate([proj_s[0], proj_s[1]], axis=1)[:, :FS].astype(BF16)
    t_s[:, 1152:] = jnp.zeros((FS, 128), BF16)
    t_s[:, :PD] = dot(grad_rows, patches_ref[...], ((0,), (0,))).astype(BF16)
    for j in range(10):
        a_own[pl.ds(10 * j, 10)] = t_s[:, 128 * j:128 * (j + 1)].reshape(10, 16, 128)
    a_own[pl.ds(100, 28)] = jnp.zeros((28, 16, 128), BF16)
    for k, peer in enumerate(x_peers):
        send(a_own.at[pl.ds(32 * wrap(x + 1 + k, X), 32)], a_xr.at[k], ax_ss.at[k], ax_rs.at[k], peer)

    g_send(2)

    total = a_own[pl.ds(32 * x, 32)].astype(F32)
    for k in range(X - 1):
        arrived(a_xr.at[k], ax_rs.at[k], sibling)
        total = total + a_xr[k].astype(F32)
    a_x[...] = total.astype(BF16)
    for k, peer in enumerate(z_peers):
        send(a_x.at[pl.ds(4 * wrap(z + 1 + k, Z), 4)], a_zr.at[k], az_ss.at[k], az_rs.at[k], peer)

    for k in range(Y - 1):
        arrived(e_recv.at[k], ey_rs.at[k], sibling)
    for k in range(QUAD):
        total = e_send[y, k].astype(F32)
        for j in range(Y - 1):
            total = total + e_recv[j, k].astype(F32)
        e_sum[k] = total.astype(BF16)
    swap_start(e_sum, e_fin, 1)

    total = a_x[pl.ds(4 * z, 4)].astype(F32)
    for k in range(Z - 1):
        arrived(a_zr.at[k], az_rs.at[k], sibling)
        total = total + a_zr[k].astype(F32)
    fin = a_all.at[pl.ds(32 * x + 4 * z, 4)]
    fin[...] = total.astype(BF16)
    for k, peer in enumerate(z_peers):
        send(fin, fin, bz_ss.at[k], bz_rs.at[k], peer)

    g_send(3)

    for k in range(Z - 1):
        arrived(a_all.at[pl.ds(32 * x + 4 * wrap(z - 1 - k, Z), 4)], bz_rs.at[k], sibling)
    fin = a_all.at[pl.ds(32 * x, 32)]
    for k, peer in enumerate(x_peers):
        send(fin, fin, bx_ss.at[k], bx_rs.at[k], peer)

    term = merge_term(z)
    for half in (0, 1):
        value = term[half * HALF:(half + 1) * HALF]
        for way in (0, 1):
            arrived(g_recv_buf.at[way, 3, half], g_rs.at[way, 3, half], sibling)
            value = value + g_recv_buf[way, 3, half].astype(F32)
        gm_ref[pl.ds(half * HALF, HALF)] = value

    swap_wait(e_sum, e_fin, 1)
    for k in range(QUAD):
        block = e_fin[k]
        embeds_ref[:, k * NC:(k + 1) * NC] = jnp.where(live_rows(NC), block, jnp.zeros_like(block))

    for k in range(X - 1):
        arrived(a_all.at[pl.ds(32 * wrap(x - 1 - k, X), 32)], bx_rs.at[k], sibling)
    for j in range(9):
        gp_ref[:, 128 * j:128 * (j + 1)] = a_all[pl.ds(10 * j, 10)].reshape(FS, 128).astype(F32)
    gp_ref[:, 1152:] = a_all[pl.ds(90, 10)].reshape(FS, 128).astype(F32)[:, :PD - 1152]

    for copy in started:
        copy.wait_send()


def body(patches, rank_groups, patch_weight, merge_weight, emb_grad):
    vmem = pl.BlockSpec(memory_space=pltpu.VMEM)
    dma = pltpu.SemaphoreType.DMA
    rows = 4 * G
    scratch = [
        pltpu.VMEM((Z, K, NC), BF16),
        pltpu.VMEM((QUAD, G, NC), BF16),
        pltpu.VMEM((QUAD, G, NC), BF16),
        pltpu.VMEM((X, Z, G, NC), BF16),
        pltpu.VMEM((X, G, K), BF16),
        pltpu.VMEM((K, X * G), BF16),
        pltpu.VMEM((2, rows, 128), F32),
        pltpu.VMEM((PD, 256), BF16),
        pltpu.VMEM((2, G, K), F32),
        pltpu.VMEM((2, T, 8, G), F32),
        pltpu.VMEM((2, 4, 2, HALF, NC), BF16),
        pltpu.VMEM((2, 4, 2, HALF, NC), BF16),
        pltpu.VMEM((X - 1, G, K), BF16),
        pltpu.VMEM((G, K), F32),
        pltpu.VMEM((X - 1, G, K), BF16),
        pltpu.VMEM((QUAD, X, G, NC), BF16),
        pltpu.VMEM((QUAD, X, G, NC), BF16),
        pltpu.VMEM((Y, QUAD, G, NC), BF16),
        pltpu.VMEM((Y - 1, QUAD, G, NC), BF16),
        pltpu.VMEM((QUAD, G, NC), BF16),
        pltpu.VMEM((QUAD, G, NC), BF16),
        pltpu.VMEM((FS, 1280), BF16),
        pltpu.VMEM((128, 16, 128), BF16),
        pltpu.VMEM((X - 1, 32, 16, 128), BF16),
        pltpu.VMEM((32, 16, 128), BF16),
        pltpu.VMEM((Z - 1, 4, 16, 128), BF16),
        pltpu.VMEM((128, 16, 128), BF16),
    ]
    for shape in (
        (2, 4, 2), (2, 4, 2), (2,), (2,), (3,), (3,), (4,), (4,), (2, 7), (2, 7), (3,), (3,),
        (3,), (3,), (2, 4, 2), (2, 4, 2), (4,), (4,), (3,), (3,), (3,), (3,), (7,), (7,),
        (7,), (7,), (3,), (3,),
    ):
        scratch.append(dma(shape))
    embeds, grad_merge, grad_patch = pl.pallas_call(
        kernel,
        out_shape=(
            jax.ShapeDtypeStruct((G, QUAD * NC), BF16),
            jax.ShapeDtypeStruct((K, NC), F32),
            jax.ShapeDtypeStruct((FS, PD), F32),
        ),
        in_specs=[pl.BlockSpec(memory_space=pltpu.SMEM)] + [vmem] * 4,
        out_specs=(vmem, vmem, vmem),
        scratch_shapes=scratch,
        compiler_params=pltpu.CompilerParams(
            collective_id=0, has_side_effects=True, vmem_limit_bytes=56 * 2**20
        ),
        name="tower",
    )(rank_groups, patches, patch_weight, merge_weight.reshape(K, NC), emb_grad)
    return embeds, grad_merge.reshape(4, FS, NC), grad_patch.T


def solution(mesh):
    return jax.shard_map(
        body,
        mesh=mesh,
        in_specs=(
            P("dp", None),
            P("dp"),
            P(None, "tensor"),
            P(None, "tensor", "dp"),
            P("dp", "tensor"),
        ),
        out_specs=(P("dp", "tensor"), P(None, "tensor", "dp"), P(None, "tensor")),
        check_vma=False,
    )
```

time: 623 us -> 172 us (0.28)
  the two profiles are of different devices: /device:TPU:1 before, /device:TPU:180 now
where the time goes in v1:
time: 172 us; the launch traced here: 171 us
  Pallas kernels  159 us (92%)
  local copies, waits for them, and re-layouts  11.2 us (7%)
    pallas_call x1, Pallas kernels, body(): pl.pallas_call(kernel, out_shape=(jax.ShapeDtypeStruct((G, QUAD * NC), BF...  159 us
    unnamed x7, local copies, waits for them, and re-layouts  11.2 us

profile of v1, /device:TPU:180, one launch (start us, length us, event | category | flops | bytes accessed | tf_op | source)
XLA Modules:
  0.0 171.4 jit_solution(12628311071007238073)
XLA Ops:
  1.3 2.1 %copy.9.pw_ref = bf16[1176,160]{1,0:T(8,128)(2,1)} copy(bf16[1176,160]{0,1:T(8,128)(2,1)} %param.7) | data formatting | bytes 752640 | tf_op args[2]
  3.3 4.3 %copy.8.patches_ref = bf16[1024,1176]{1,0:T(8,128)(2,1)} copy(bf16[1024,1176]{0,1:T(8,128)(2,1)} %param.5) | data formatting | bytes 4816896 | tf_op args[0]
  7.7 158.9 %tower.1 = (bf16[256,1024]{1,0:T(8,128)(2,1)}, f32[640,256]{1,0:T(8,128)}, f32[160,1176]{1,0:T(8,128)}) custom-call(s32[1]{0:T(128)S(6)} %copy.13.live_ref, bf16[1024,1176]{1,0:T(8,128)(2,1)} %copy.8.patches_ref, bf16[1176,160]{1,0:T(8,128)(2,1)} %copy.9.pw_ref, bf16[640,256]{1,0:T(8,128)(2,1)} %bitcast.5, bf16[256,1024]{1,0:T(8,128)(2,1)} %emb_ref.1), custom_call_target="tpu_custom_call" | custom-call | tf_op jit(solution)/shard_map/tower/pallas_call | solution.py:416
  166.5 0.0 copy-start
  166.6 1.9 %copy.14 = bf16[256,1024]{1,0:T(8,128)(2,1)} copy(bf16[256,1024]{1,0:T(8,128)(2,1)} %get-tuple-element.12) | data formatting | bytes 1048576
  168.5 2.0 %copy.15 = f32[4,160,256]{2,1,0:T(8,128)} copy(f32[4,160,256]{2,1,0:T(8,128)} %bitcast.4) | data formatting | bytes 1310720
  170.5 0.0 copy-done
  170.5 0.9 copy.16
Async XLA Ops:
  166.5 3.9 %copy-start = (f32[160,1176]{1,0:T(8,128)S(1)}, f32[160,1176]{1,0:T(8,128)}, u32[]{:S(2)}) copy-start(f32[160,1176]{1,0:T(8,128)} %get-tuple-element.8) | copy-start | bytes 2257924

commit v2 on v1

v2 whole, which is shorter than its diff:
```python
import functools

import jax
import jax.numpy as jnp
from jax import lax
from jax.experimental import pallas as pl
from jax.experimental.pallas import tpu as pltpu
from jax.sharding import PartitionSpec as P

E = 1280
X, Y, Z = 4, 4, 8
T = 2 * Y
F32, BF16 = jnp.float32, jnp.bfloat16
HIGH = lax.Precision.HIGHEST

PD = 1176
FS = E // T
K = 4 * FS
G = 256
NC = 256
HALF = K // 2
QUAD = Z // 2


def dot(a, b, dims=((1,), (0,)), precision=None):
    return lax.dot_general(a, b, (dims, ((), ())), precision=precision, preferred_element_type=F32)


def wrap(value, count):
    return lax.rem(value + count, count)


def group_rows(offset):
    row = lax.broadcasted_iota(jnp.int32, (8, K), 0)
    lane = lax.broadcasted_iota(jnp.int32, (8, K), 1)
    low = (row - offset) * FS
    return jnp.where((lane >= low) & (lane < low + FS), 1.0, 0.0).astype(F32)


def kernel(
    live_ref, patches_hbm, pw_hbm, w_hbm, emb_hbm,
    embeds_ref, gm_ref, gp_ref,
    patches_ref, pw_ref, emb_ref,
    wg, cot_own, cot_p1, cot_all, merged_all, merged_t, proj_s, normed_s,
    stats, g_send_buf, g_recv_buf, d_send_buf, d_own, d_recv_buf,
    e_sib_send, e_sib_recv, e_send, e_recv, e_sum, e_p2, e_fin,
    t_s, a_own, a_xr, a_x, a_zr, a_all,
    in_s,
    w_ss, w_rs, p1_ss, p1_rs, p2_ss, p2_rs, p3_ss, p3_rs, cs_ss, cs_rs,
    st_ss, st_rs, m_ss, m_rs,
    d_ss, d_rs, g_ss, g_rs, es_ss, es_rs, ey_ss, ey_rs, e2_ss, e2_rs, e1_ss, e1_rs,
    ax_ss, ax_rs, az_ss, az_rs, bz_ss, bz_rs, bx_ss, bx_rs,
):
    dp = lax.axis_index("dp")
    t = lax.axis_index("tensor")
    x, z = lax.div(dp, Z), lax.rem(dp, Z)
    y, c = lax.div(t, 2), lax.rem(t, 2)

    def device(x, y, z, c):
        return (x * Z + z, y * 2 + c)

    started = []

    def send(src, dst, ssem, rsem, to):
        copy = pltpu.make_async_remote_copy(
            src_ref=src, dst_ref=dst, send_sem=ssem, recv_sem=rsem,
            device_id=to, device_id_type=pl.DeviceIdType.MESH,
        )
        copy.start()
        started.append(copy)

    def arrived(dst, rsem):
        pltpu.make_async_remote_copy(
            src_ref=dst, dst_ref=dst, send_sem=w_ss.at[0, 0, 0], recv_sem=rsem,
            device_id=sibling, device_id_type=pl.DeviceIdType.MESH,
        ).wait_recv()

    right = device(x, y, wrap(z + 1, Z), c)
    left = device(x, y, wrap(z - 1, Z), c)
    sibling = device(x, y, z, 1 - c)
    xs = [wrap(x + k, X) for k in range(X)]
    ys = [wrap(y + k, Y) for k in range(Y)]
    zs = [wrap(z + k, Z) for k in range(Z)]
    x_peers = [device(i, y, z, c) for i in xs]
    y_peers = [device(x, i, z, c) for i in ys]
    z_peers = [device(x, y, i, c) for i in zs]
    t_peers = [(dp, wrap(t + k, T)) for k in range(T)]

    inputs = [
        pltpu.make_async_copy(w_hbm, wg.at[z], in_s.at[0]),
        pltpu.make_async_copy(emb_hbm, emb_ref, in_s.at[1]),
        pltpu.make_async_copy(pw_hbm, pw_ref, in_s.at[2]),
        pltpu.make_async_copy(patches_hbm, patches_ref, in_s.at[3]),
    ]
    for copy in inputs:
        copy.start()

    barrier = pltpu.get_barrier_semaphore()
    greeted = x_peers[1:] + z_peers[1:] + t_peers[1:]
    for peer in greeted:
        pl.semaphore_signal(barrier, inc=1, device_id=peer, device_id_type=pl.DeviceIdType.MESH)

    inputs[0].wait()
    inputs[1].wait()
    live = live_ref[0]
    live_rows = lax.broadcasted_iota(jnp.int32, (G, NC), 0) < live
    for k in range(QUAD):
        block = emb_ref[:, k * NC:(k + 1) * NC]
        cot_own[k] = jnp.where(live_rows, block, jnp.zeros_like(block))

    pl.semaphore_wait(barrier, len(greeted))

    for k in range(1, Y):
        send(cot_own.at[ys[k]], cot_p1.at[y], p1_ss.at[k], p1_rs.at[y], y_peers[k])

    def w_part(index, half):
        return wg.at[index, pl.ds(half * HALF, HALF)]

    def w_send(step):
        for way, to, block in ((0, right, wrap(z - step, Z)), (1, left, wrap(z + step, Z))):
            for half in (0, 1) if step < 3 else (way,):
                part = w_part(block, half)
                if step:
                    arrived(part, w_rs.at[way, step - 1, half])
                send(part, part, w_ss.at[way, step, half], w_rs.at[way, step, half], to)

    def w_finish():
        for way, block in ((0, wrap(z - 3, Z)), (1, wrap(z + 3, Z))):
            arrived(w_part(block, 1 - way), w_rs.at[way, 2, 1 - way])
        for way in (0, 1):
            arrived(w_part(wrap(z + 4, Z), way), w_rs.at[way, 3, way])

    w_send(0)
    cot_p1[y] = cot_own[y]

    inputs[2].wait()
    inputs[3].wait()
    for i in range(4):
        rows = pl.ds(i * 256, 256)
        product = dot(pw_ref[...], patches_ref[:, i * 256:(i + 1) * 256])
        product = jnp.transpose(jnp.concatenate([product, jnp.zeros((256 - FS, 256), F32)], axis=0))
        proj_s[0, rows] = product[:, :128]
        proj_s[1, rows] = product[:, 128:]

    parts = []
    for q in range(4):
        rows = pl.ds(q, G, stride=4)
        parts.append(jnp.concatenate([proj_s[0, rows, :], proj_s[1, rows, :]], axis=1)[:, :FS])
    projected = jnp.concatenate(parts, axis=1)

    first, second = group_rows(0), group_rows(4)

    def sums_over_tensor(index, one, two):
        stats[index, t] = (
            dot(first, one, ((1,), (1,)), HIGH) + dot(second, two, ((1,), (1,)), HIGH)
        )
        mine = stats.at[index, t]
        for k in range(1, T):
            send(mine, mine, st_ss.at[index, k], st_rs.at[index, t], t_peers[k])

    def totals(index):
        for k in range(1, T):
            owner = wrap(t + k, T)
            arrived(stats.at[index, owner], st_rs.at[index, owner])
        total = stats[index, 0]
        for k in range(1, T):
            total = total + stats[index, k]
        return total / E

    def spread(rows, value):
        return dot(value, rows, ((0,), (0,)), HIGH)

    sums_over_tensor(0, projected, projected * projected)

    for k in (1, 2, 3, 0):
        origin = xs[k]
        block = cot_p1.at[origin]

        @pl.when(origin != y)
        def _():
            arrived(block, p1_rs.at[origin])

        slot = cot_all.at[x, c * QUAD + y]
        if k:
            send(block, slot, p2_ss.at[k], p2_rs.at[x], x_peers[k])
        else:
            slot[...] = block[...]

    def cot_out(k):
        block = cot_all.at[xs[k], c * QUAD + y]
        if k:
            arrived(block, p2_rs.at[xs[k]])
        for j in range(1, Y):
            send(block, block, p3_ss.at[k, j], p3_rs.at[xs[k], y], y_peers[j])
        send(block, block, cs_ss.at[k, 0], cs_rs.at[xs[k], y], sibling)

    def cot_on(k):
        for j in range(1, Y):
            block = cot_all.at[xs[k], c * QUAD + ys[j]]
            arrived(block, p3_rs.at[xs[k], ys[j]])
            send(block, block, cs_ss.at[k, j], cs_rs.at[xs[k], ys[j]], sibling)

    def cot_in(k):
        for j in range(Y):
            arrived(cot_all.at[xs[k], (1 - c) * QUAD + ys[j]], cs_rs.at[xs[k], ys[j]])

    cot_out(0)

    means = totals(0)
    row = lax.broadcasted_iota(jnp.int32, (8, G), 0)
    row_mean = pltpu.roll(means, 4, 0)
    inv_scale = jnp.where(row >= 4, lax.rsqrt(
        jnp.where(row >= 4, means - row_mean * row_mean, 1.0) + 1e-05), 0.0)
    inv_wide = spread(second, inv_scale)
    normed = (projected - spread(first, means)) * inv_wide
    normed_s[0] = normed
    normed_s[1] = inv_wide
    merged_all[x] = normed.astype(BF16)
    for k in range(1, X):
        send(merged_all.at[x], merged_all.at[x], m_ss.at[k], m_rs.at[x], x_peers[k])

    w_send(1)
    for k in (1, 2, 3):
        cot_out(k)
    merged_t[:, pl.ds(x * G, G)] = jnp.transpose(merged_all[x])
    cot_on(0)
    w_send(2)
    cot_on(1)
    w_send(3)
    for k in range(1, X):
        arrived(merged_all.at[xs[k]], m_rs.at[xs[k]])
        merged_t[:, pl.ds(xs[k] * G, G)] = jnp.transpose(merged_all[xs[k]])
    cot_on(2)
    w_finish()

    def d_term(owner):
        total = None
        for block in range(Z):
            term = dot(cot_all[owner, block], wg[block], ((1,), (1,)))
            total = term if total is None else total + term
        return total

    def d_send(k):
        d_send_buf[k] = d_term(xs[k]).astype(BF16)
        send(d_send_buf.at[k], d_recv_buf.at[x], d_ss.at[k], d_rs.at[x], x_peers[k])

    cot_in(1)
    d_send(1)
    cot_on(3)
    cot_in(2)
    d_send(2)

    for k in range(QUAD):
        block = wg[(1 - c) * QUAD + ys[(k + 1) % Y]]
        for i in range(X):
            e_sib_send[k, i] = dot(merged_all[i], block).astype(BF16)
        send(e_sib_send.at[k], e_sib_recv.at[k], es_ss.at[k], es_rs.at[k], sibling)

    cot_in(3)
    d_send(3)
    cot_in(0)

    def merge_term(block):
        return dot(merged_t[...], cot_all[:, block].reshape(X * G, NC))

    def g_send(step):
        for way, to, block in ((0, right, wrap(z + 4 - step, Z)), (1, left, wrap(z - 4 + step, Z))):
            term = merge_term(block)
            for half in (0, 1) if step else (way,):
                value = term[half * HALF:(half + 1) * HALF]
                if step > 1 or (step == 1 and half == way):
                    arrived(g_recv_buf.at[way, step - 1, half], g_rs.at[way, step - 1, half])
                    value = value + g_recv_buf[way, step - 1, half].astype(F32)
                g_send_buf[way, step, half] = value.astype(BF16)
                send(g_send_buf.at[way, step, half], g_recv_buf.at[way, step, half],
                     g_ss.at[way, step, half], g_rs.at[way, step, half], to)

    g_send(0)

    d_own[...] = d_term(x)

    for k in range(QUAD):
        target = (k + 1) % Y
        block = wg[c * QUAD + ys[target]]
        arrived(e_sib_recv.at[k], es_rs.at[k])
        for i in range(X):
            value = dot(merged_all[i], block) + e_sib_recv[k, i].astype(F32)
            e_send[k, i] = value.astype(BF16)
        if target:
            send(e_send.at[k], e_recv.at[y], ey_ss.at[k], ey_rs.at[y], y_peers[target])

    g_send(1)

    dnormed = d_own[...]
    for k in range(1, X):
        arrived(d_recv_buf.at[xs[k]], d_rs.at[xs[k]])
        dnormed = dnormed + d_recv_buf[xs[k]].astype(F32)
    normed = normed_s[0]
    sums_over_tensor(1, dnormed, dnormed * normed)
    d_own[...] = dnormed

    g_send(2)

    means = totals(1)
    d_mean = spread(first, means)
    dn_mean = spread(second, means)
    grad_input = (d_own[...] - d_mean - normed_s[0] * dn_mean) * normed_s[1]
    for q in range(4):
        part = grad_input[:, q * FS:(q + 1) * FS]
        part = jnp.concatenate([part, jnp.zeros((G, 256 - FS), F32)], axis=1)
        rows = pl.ds(q, G, stride=4)
        proj_s[0, rows, :] = part[:, :128]
        proj_s[1, rows, :] = part[:, 128:]
    grad_rows = jnp.concatenate([proj_s[0], proj_s[1]], axis=1)
    grad_rows = jnp.transpose(grad_rows)[:FS].astype(BF16)
    t_s[:, 1152:] = jnp.zeros((FS, 128), BF16)
    t_s[:, :PD] = dot(grad_rows, patches_ref[...], ((1,), (1,))).astype(BF16)
    for j in range(10):
        a_own[pl.ds(10 * j, 10)] = t_s[:, 128 * j:128 * (j + 1)].reshape(10, 16, 128)
    a_own[pl.ds(100, 28)] = jnp.zeros((28, 16, 128), BF16)
    for k in range(1, X):
        send(a_own.at[pl.ds(32 * xs[k], 32)], a_xr.at[x], ax_ss.at[k], ax_rs.at[x], x_peers[k])

    for k in range(1, Y):
        arrived(e_recv.at[ys[k]], ey_rs.at[ys[k]])
    for k in (1, 2, 3, 0):
        total = e_send[QUAD - 1, xs[k]].astype(F32)
        for j in range(1, Y):
            total = total + e_recv[ys[j], xs[k]].astype(F32)
        total = total.astype(BF16)
        if k:
            e_sum[k] = total
            send(e_sum.at[k], e_p2.at[x], e2_ss.at[k], e2_rs.at[x], x_peers[k])
        else:
            e_p2[x] = total

    total = a_own[pl.ds(32 * x, 32)].astype(F32)
    for k in range(1, X):
        arrived(a_xr.at[xs[k]], ax_rs.at[xs[k]])
        total = total + a_xr[xs[k]].astype(F32)
    a_x[...] = total.astype(BF16)
    for k in range(1, Z):
        send(a_x.at[pl.ds(4 * zs[k], 4)], a_zr.at[z], az_ss.at[k], az_rs.at[z], z_peers[k])

    for k in (1, 2, 3, 0):
        origin = ys[k]
        block = e_p2.at[origin]

        @pl.when(origin != x)
        def _():
            arrived(block, e2_rs.at[origin])

        if k:
            send(block, e_fin.at[y], e1_ss.at[k], e1_rs.at[y], y_peers[k])
        else:
            e_fin[y] = block[...]

    total = a_x[pl.ds(4 * z, 4)].astype(F32)
    for k in range(1, Z):
        arrived(a_zr.at[zs[k]], az_rs.at[zs[k]])
        total = total + a_zr[zs[k]].astype(F32)
    fin = a_all.at[pl.ds(32 * x + 4 * z, 4)]
    fin[...] = total.astype(BF16)
    for k in range(1, Z):
        send(fin, fin, bz_ss.at[k], bz_rs.at[z], z_peers[k])

    g_send(3)

    for k in range(1, Z):
        arrived(a_all.at[pl.ds(32 * x + 4 * zs[k], 4)], bz_rs.at[zs[k]])
    fin = a_all.at[pl.ds(32 * x, 32)]
    for k in range(1, X):
        send(fin, fin, bx_ss.at[k], bx_rs.at[x], x_peers[k])

    term = merge_term(z)
    for half in (0, 1):
        value = term[half * HALF:(half + 1) * HALF]
        for way in (0, 1):
            arrived(g_recv_buf.at[way, 3, half], g_rs.at[way, 3, half])
            value = value + g_recv_buf[way, 3, half].astype(F32)
        gm_ref[pl.ds(half * HALF, HALF)] = value

    for k in range(1, Y):
        arrived(e_fin.at[ys[k]], e1_rs.at[ys[k]])
    for k in range(QUAD):
        block = e_fin[k]
        embeds_ref[:, k * NC:(k + 1) * NC] = jnp.where(live_rows, block, jnp.zeros_like(block))

    for k in range(1, X):
        arrived(a_all.at[pl.ds(32 * xs[k], 32)], bx_rs.at[xs[k]])
    for j in range(9):
        gp_ref[:, 128 * j:128 * (j + 1)] = a_all[pl.ds(10 * j, 10)].reshape(FS, 128).astype(F32)
    gp_ref[:, 1152:] = a_all[pl.ds(90, 10)].reshape(FS, 128).astype(F32)[:, :PD - 1152]

    for copy in started:
        copy.wait_send()


def body(patches, rank_groups, patch_weight, merge_weight, emb_grad):
    vmem = pl.BlockSpec(memory_space=pltpu.VMEM)
    dma = pltpu.SemaphoreType.DMA
    rows = 4 * G
    scratch = [
        pltpu.VMEM((PD, rows), BF16),
        pltpu.VMEM((FS, PD), BF16),
        pltpu.VMEM((G, QUAD * NC), BF16),
        pltpu.VMEM((Z, K, NC), BF16),
        pltpu.VMEM((QUAD, G, NC), BF16),
        pltpu.VMEM((Y, G, NC), BF16),
        pltpu.VMEM((X, Z, G, NC), BF16),
        pltpu.VMEM((X, G, K), BF16),
        pltpu.VMEM((K, X * G), BF16),
        pltpu.VMEM((2, rows, 128), F32),
        pltpu.VMEM((2, G, K), F32),
        pltpu.VMEM((2, T, 8, G), F32),
        pltpu.VMEM((2, 4, 2, HALF, NC), BF16),
        pltpu.VMEM((2, 4, 2, HALF, NC), BF16),
        pltpu.VMEM((X, G, K), BF16),
        pltpu.VMEM((G, K), F32),
        pltpu.VMEM((X, G, K), BF16),
        pltpu.VMEM((QUAD, X, G, NC), BF16),
        pltpu.VMEM((QUAD, X, G, NC), BF16),
        pltpu.VMEM((QUAD, X, G, NC), BF16),
        pltpu.VMEM((Y, X, G, NC), BF16),
        pltpu.VMEM((X, G, NC), BF16),
        pltpu.VMEM((X, G, NC), BF16),
        pltpu.VMEM((QUAD, G, NC), BF16),
        pltpu.VMEM((FS, 1280), BF16),
        pltpu.VMEM((128, 16, 128), BF16),
        pltpu.VMEM((X, 32, 16, 128), BF16),
        pltpu.VMEM((32, 16, 128), BF16),
        pltpu.VMEM((Z, 4, 16, 128), BF16),
        pltpu.VMEM((128, 16, 128), BF16),
        dma((4,)),
    ]
    for shape in (
        (2, 4, 2), (4,), (4,), (4, 4), (4, 4), (2, 8), (4,),
        (4,), (2, 4, 2), (4,), (4,), (4,), (4,), (4,), (8,), (8,), (4,),
    ):
        scratch += [dma(shape), dma(shape)]
    embeds, grad_merge, grad_patch = pl.pallas_call(
        kernel,
        out_shape=(
            jax.ShapeDtypeStruct((G, QUAD * NC), BF16),
            jax.ShapeDtypeStruct((K, NC), F32),
            jax.ShapeDtypeStruct((FS, PD), F32),
        ),
        in_specs=[pl.BlockSpec(memory_space=pltpu.SMEM)] + [pl.BlockSpec(memory_space=pl.ANY)] * 4,
        out_specs=(vmem, vmem, vmem),
        scratch_shapes=scratch,
        compiler_params=pltpu.CompilerParams(
            collective_id=0, has_side_effects=True, vmem_limit_bytes=56 * 2**20
        ),
        name="tower",
    )(rank_groups, patches.T, patch_weight.T, merge_weight.reshape(K, NC), emb_grad)
    return embeds, grad_merge.reshape(4, FS, NC), grad_patch.T


def solution(mesh):
    return jax.shard_map(
        body,
        mesh=mesh,
        in_specs=(
            P("dp", None),
            P("dp"),
            P(None, "tensor"),
            P(None, "tensor", "dp"),
            P("dp", "tensor"),
        ),
        out_specs=(P("dp", "tensor"), P(None, "tensor", "dp"), P(None, "tensor")),
        check_vma=False,
    )
```

time: 172 us -> 117 us (0.68)
  the two profiles are of different devices: /device:TPU:180 before, /device:TPU:1 now
where the time goes in v2:
time: 117 us
  Pallas kernels  111 us (95%)
  local copies, waits for them, and re-layouts  4.82 us (4%)
  between operations  1.29 us (1%)
    pallas_call x1, Pallas kernels, body(): pl.pallas_call(kernel, out_shape=(jax.ShapeDtypeStruct((G, QUAD * NC), BF...  111 us
    unnamed x5, local copies, waits for them, and re-layouts  4.82 us

profile of v2, /device:TPU:1, one launch (start us, length us, event | category | flops | bytes accessed | tf_op | source)
XLA Modules:
  0.0 117.1 jit_solution(16066266863889368180)
XLA Ops:
  1.3 111.0 %tower.1 = (bf16[256,1024]{1,0:T(8,128)(2,1)}, f32[640,256]{1,0:T(8,128)}, f32[160,1176]{1,0:T(8,128)}) custom-call(s32[1]{0:T(128)S(6)} %copy.11.live_ref, bf16[1176,1024]{1,0:T(8,128)(2,1)} %bitcast.5, bf16[160,1176]{1,0:T(8,128)(2,1)} %bitcast.8, bf16[640,256]{1,0:T(8,128)(2,1)} %bitcast.9, bf16[256,1024]{1,0:T(8,128)(2,1)} %emb_hbm.1), custom_call_target="tpu_custom_call" | custom-call | tf_op jit(solution)/shard_map/tower/pallas_call | solution.py:441
  112.3 0.0 copy-start
  112.3 1.9 %copy.12 = bf16[256,1024]{1,0:T(8,128)(2,1)} copy(bf16[256,1024]{1,0:T(8,128)(2,1)} %get-tuple-element.12) | data formatting | bytes 1048576
  114.2 2.0 %copy.13 = f32[4,160,256]{2,1,0:T(8,128)} copy(f32[4,160,256]{2,1,0:T(8,128)} %bitcast.7) | data formatting | bytes 1310720
  116.2 0.0 copy-done
  116.2 0.9 copy.14
Async XLA Ops:
  112.3 3.9 %copy-start = (f32[160,1176]{1,0:T(8,128)S(1)}, f32[160,1176]{1,0:T(8,128)}, u32[]{:S(2)}) copy-start(f32[160,1176]{1,0:T(8,128)} %get-tuple-element.8) | copy-start | bytes 2257924

commit v3 on v2

v3 whole, which is shorter than its diff:
```python
import functools

import jax
import jax.numpy as jnp
from jax import lax
from jax.experimental import pallas as pl
from jax.experimental.pallas import tpu as pltpu
from jax.sharding import PartitionSpec as P

E = 1280
X, Y, Z = 4, 4, 8
T = 2 * Y
F32, BF16 = jnp.float32, jnp.bfloat16
HIGH = lax.Precision.HIGHEST

PD = 1176
FS = E // T
K = 4 * FS
G = 256
NC = 256
HALF = K // 2
QUAD = Z // 2


def dot(a, b, dims=((1,), (0,)), precision=None):
    return lax.dot_general(a, b, (dims, ((), ())), precision=precision, preferred_element_type=F32)


def wrap(value, count):
    return lax.rem(value + count, count)


def group_rows(offset):
    row = lax.broadcasted_iota(jnp.int32, (8, K), 0)
    lane = lax.broadcasted_iota(jnp.int32, (8, K), 1)
    low = (row - offset) * FS
    return jnp.where((lane >= low) & (lane < low + FS), 1.0, 0.0).astype(F32)


def kernel(
    live_ref, patches_hbm, pw_hbm, w_hbm, emb_hbm,
    embeds_hbm, gm_hbm, gp_hbm,
    embeds_ref, gm_ref, gp_ref,
    patches_ref, pw_ref, emb_ref,
    wg, cot_own, cot_p1, cot_all, merged_all, merged_t, proj_s, normed_s,
    stats, sx_send, sx_recv, g_send_buf, g_recv_buf, d_send_buf, d_own, d_recv_buf,
    e_sib_send, e_sib_recv, e_send, e_recv, e_sum, e_p2, e_fin,
    t_s, a_own, a_xr, a_x, a_zr, a_all,
    in_s, out_s,
    w_ss, w_rs, p1_ss, p1_rs, p2_ss, p2_rs, p3_ss, p3_rs, ph_ss, ph_rs, cs_ss, cs_rs,
    st_ss, st_rs, sx_ss, sx_rs, m_ss, m_rs,
    d_ss, d_rs, g_ss, g_rs, es_ss, es_rs, ey_ss, ey_rs, e2_ss, e2_rs, e1_ss, e1_rs,
    ax_ss, ax_rs, az_ss, az_rs, bz_ss, bz_rs, bx_ss, bx_rs,
):
    dp = lax.axis_index("dp")
    t = lax.axis_index("tensor")
    x, z = lax.div(dp, Z), lax.rem(dp, Z)
    y, c = lax.div(t, 2), lax.rem(t, 2)

    def device(x, y, z, c):
        return (x * Z + z, y * 2 + c)

    started = []

    def send(src, dst, ssem, rsem, to):
        copy = pltpu.make_async_remote_copy(
            src_ref=src, dst_ref=dst, send_sem=ssem, recv_sem=rsem,
            device_id=to, device_id_type=pl.DeviceIdType.MESH,
        )
        copy.start()
        started.append(copy)

    def arrived(dst, rsem):
        pltpu.make_async_remote_copy(
            src_ref=dst, dst_ref=dst, send_sem=w_ss.at[0, 0, 0], recv_sem=rsem,
            device_id=sibling, device_id_type=pl.DeviceIdType.MESH,
        ).wait_recv()

    right = device(x, y, wrap(z + 1, Z), c)
    left = device(x, y, wrap(z - 1, Z), c)
    sibling = device(x, y, z, 1 - c)
    xs = [wrap(x + k, X) for k in range(X)]
    ys = [wrap(y + k, Y) for k in range(Y)]
    zs = [wrap(z + k, Z) for k in range(Z)]
    x_peers = [device(i, y, z, c) for i in xs]
    y_peers = [device(x, i, z, c) for i in ys]
    z_peers = [device(x, y, i, c) for i in zs]
    t_peers = [(dp, wrap(t + k, T)) for k in range(T)]

    inputs = [
        pltpu.make_async_copy(w_hbm, wg.at[z], in_s.at[0]),
        pltpu.make_async_copy(emb_hbm, emb_ref, in_s.at[1]),
        pltpu.make_async_copy(pw_hbm, pw_ref, in_s.at[2]),
        pltpu.make_async_copy(patches_hbm, patches_ref, in_s.at[3]),
    ]
    for copy in inputs:
        copy.start()

    barrier = pltpu.get_barrier_semaphore()
    greeted = x_peers[1:] + z_peers[1:] + t_peers[1:]
    for peer in greeted:
        pl.semaphore_signal(barrier, inc=1, device_id=peer, device_id_type=pl.DeviceIdType.MESH)

    inputs[0].wait()
    inputs[1].wait()
    live = live_ref[0]
    live_rows = lax.broadcasted_iota(jnp.int32, (G, NC), 0) < live
    for k in range(QUAD):
        block = emb_ref[:, k * NC:(k + 1) * NC]
        cot_own[k] = jnp.where(live_rows, block, jnp.zeros_like(block))

    pl.semaphore_wait(barrier, len(greeted))

    for k in range(1, Y):
        send(cot_own.at[ys[k]], cot_p1.at[y], p1_ss.at[k], p1_rs.at[y], y_peers[k])

    def w_part(index, half):
        return wg.at[index, pl.ds(half * HALF, HALF)]

    def w_fwd(step, piece):
        for way, to, block in ((0, right, wrap(z - step, Z)), (1, left, wrap(z + step, Z))):
            half = piece if way == 0 else 1 - piece
            part = w_part(block, half)
            if step:
                arrived(part, w_rs.at[way, step - 1, half])
            send(part, part, w_ss.at[way, step, half], w_rs.at[way, step, half], to)

    def w_finish():
        for way, block in ((0, wrap(z - 3, Z)), (1, wrap(z + 3, Z))):
            arrived(w_part(block, 1 - way), w_rs.at[way, 2, 1 - way])
        for way in (0, 1):
            arrived(w_part(wrap(z + 4, Z), way), w_rs.at[way, 3, way])

    w_fwd(0, 0)
    w_fwd(0, 1)
    cot_p1[y] = cot_own[y]

    inputs[2].wait()
    inputs[3].wait()
    for i in range(4):
        rows = pl.ds(i * 256, 256)
        product = dot(pw_ref[...], patches_ref[:, i * 256:(i + 1) * 256])
        product = jnp.transpose(jnp.concatenate([product, jnp.zeros((256 - FS, 256), F32)], axis=0))
        proj_s[0, rows] = product[:, :128]
        proj_s[1, rows] = product[:, 128:]

    parts = []
    for q in range(4):
        rows = pl.ds(q, G, stride=4)
        parts.append(jnp.concatenate([proj_s[0, rows, :], proj_s[1, rows, :]], axis=1)[:, :FS])
    projected = jnp.concatenate(parts, axis=1)

    first, second = group_rows(0), group_rows(4)

    def send_stats(index):
        mine = stats.at[index, t]
        for k in range(1, T):
            send(mine, mine, st_ss.at[index, k], st_rs.at[index, t], t_peers[k])

    def totals(index):
        for k in range(1, T):
            owner = wrap(t + k, T)
            arrived(stats.at[index, owner], st_rs.at[index, owner])
        total = stats[index, 0]
        for k in range(1, T):
            total = total + stats[index, k]
        return total / E

    def spread(rows, value):
        return dot(value, rows, ((0,), (0,)), HIGH)

    stats[0, t] = (
        dot(first, projected, ((1,), (1,)), HIGH)
        + dot(second, projected * projected, ((1,), (1,)), HIGH)
    )
    send_stats(0)
    w_fwd(1, 0)

    for k in (1, 3, 2, 0):
        origin = xs[k]
        block = cot_p1.at[origin]

        @pl.when(origin != y)
        def _():
            arrived(block, p1_rs.at[origin])

        slot = cot_all.at[x, c * QUAD + y]
        if k:
            send(block, slot, p2_ss.at[k], p2_rs.at[x], x_peers[k])
        else:
            slot[...] = block[...]

    def cot_block(k, j):
        return cot_all.at[xs[k], c * QUAD + ys[j]]

    def to_sibling(k, j):
        block = cot_block(k, j)
        send(block, block, cs_ss.at[k, j], cs_rs.at[xs[k], ys[j]], sibling)

    def cot_out(k):
        block = cot_block(k, 0)
        if k:
            arrived(block, p2_rs.at[xs[k]])
        for j in (1, 3):
            send(block, block, p3_ss.at[k, j], p3_rs.at[xs[k], y], y_peers[j])
        to_sibling(k, 0)

    def cot_on(k):
        for half, j in ((0, 1), (1, 3)):
            block = cot_block(k, j)
            arrived(block, p3_rs.at[xs[k], ys[j]])
            part = block.at[pl.ds(half * 128, 128)]
            send(part, part, ph_ss.at[k, half], ph_rs.at[xs[k], half], y_peers[4 - j])
        to_sibling(k, 1)
        to_sibling(k, 3)

    def cot_far(k):
        for half in (0, 1):
            arrived(cot_block(k, 2).at[pl.ds(half * 128, 128)], ph_rs.at[xs[k], half])
        to_sibling(k, 2)

    def cot_in(k):
        for j in range(Y):
            arrived(cot_all.at[xs[k], (1 - c) * QUAD + ys[j]], cs_rs.at[xs[k], ys[j]])

    cot_out(0)
    w_fwd(1, 1)

    means = totals(0)
    row = lax.broadcasted_iota(jnp.int32, (8, G), 0)
    row_mean = pltpu.roll(means, 4, 0)
    inv_scale = jnp.where(row >= 4, lax.rsqrt(
        jnp.where(row >= 4, means - row_mean * row_mean, 1.0) + 1e-05), 0.0)
    inv_wide = spread(second, inv_scale)
    normed = (projected - spread(first, means)) * inv_wide
    normed_s[0] = normed
    normed_s[1] = inv_wide
    merged_all[x] = normed.astype(BF16)
    for k in range(1, X):
        send(merged_all.at[x], merged_all.at[x], m_ss.at[k], m_rs.at[x], x_peers[k])

    w_fwd(2, 0)
    cot_out(1)
    cot_out(3)
    cot_out(2)
    cot_on(0)
    w_fwd(2, 1)
    merged_t[:, pl.ds(x * G, G)] = jnp.transpose(merged_all[x])
    cot_far(0)
    cot_on(1)
    w_fwd(3, 0)
    cot_on(3)
    cot_far(1)
    cot_on(2)
    cot_far(3)
    for k in range(1, X):
        arrived(merged_all.at[xs[k]], m_rs.at[xs[k]])
        merged_t[:, pl.ds(xs[k] * G, G)] = jnp.transpose(merged_all[xs[k]])
    cot_far(2)
    for k in (0, 1, 3, 2):
        cot_in(k)

    def merge_term(block, rows=slice(None)):
        return dot(merged_t[rows], cot_all[:, block].reshape(X * G, NC))

    def g_block(way, step):
        return wrap(z + 4 - step, Z) if way == 0 else wrap(z - 4 + step, Z)

    def g_out(way, step, half, value):
        g_send_buf[way, step, half] = value.astype(BF16)
        send(g_send_buf.at[way, step, half], g_recv_buf.at[way, step, half],
             g_ss.at[way, step, half], g_rs.at[way, step, half], right if way == 0 else left)

    def g_in(way, step, half):
        arrived(g_recv_buf.at[way, step, half], g_rs.at[way, step, half])
        return g_recv_buf[way, step, half].astype(F32)

    def half_rows(half):
        return slice(half * HALF, (half + 1) * HALF)

    for way in (0, 1):
        g_out(way, 0, way, merge_term(g_block(way, 0), half_rows(way)))
    for way in (0, 1):
        g_out(way, 1, 1 - way, merge_term(g_block(way, 1), half_rows(1 - way)))

    def g_step(step):
        terms = [merge_term(g_block(way, step)) for way in (0, 1)]
        for piece in (0, 1):
            for way in (0, 1):
                half = 1 - way if piece == 0 else way
                g_out(way, step, half, terms[way][half_rows(half)] + g_in(way, step - 1, half))

    w_finish()

    def d_term(owner):
        total = None
        for block in range(Z):
            term = dot(cot_all[owner, block], wg[block], ((1,), (1,)))
            total = term if total is None else total + term
        return total

    def d_sums(term, owner):
        rounded = term.astype(BF16)
        product = (term * merged_all[owner].astype(F32)).astype(BF16)
        return (dot(first.astype(BF16), rounded, ((1,), (1,)))
                + dot(second.astype(BF16), product, ((1,), (1,))))

    for k in (1, 3, 2):
        term = d_term(xs[k])
        d_send_buf[k] = term.astype(BF16)
        sx_send[k] = d_sums(term, xs[k])
        send(sx_send.at[k], sx_recv.at[x], sx_ss.at[k], sx_rs.at[x], x_peers[k])
    for k in (1, 3, 2):
        send(d_send_buf.at[k], d_recv_buf.at[x], d_ss.at[k], d_rs.at[x], x_peers[k])

    for n in range(X):
        rows = merged_all[xs[(n + 1) % X]]
        for m in range(QUAD):
            block = wg[(1 - c) * QUAD + ys[(m + 1) % Y]]
            e_sib_send[n, m] = dot(rows, block).astype(BF16)
        send(e_sib_send.at[n], e_sib_recv.at[n], es_ss.at[n], es_rs.at[n], sibling)

    def e_out(n):
        rows = merged_all[xs[(n + 1) % X]]
        arrived(e_sib_recv.at[n], es_rs.at[n])
        for m in range(QUAD):
            value = dot(rows, wg[c * QUAD + ys[(m + 1) % Y]]) + e_sib_recv[n, m].astype(F32)
            e_send[n, m] = value.astype(BF16)
            if m < QUAD - 1:
                send(e_send.at[n, m], e_recv.at[y, n], ey_ss.at[n, m], ey_rs.at[y, n], y_peers[m + 1])

    def e_sum_up(n):
        total = e_send[n, QUAD - 1].astype(F32)
        for j in range(1, Y):
            arrived(e_recv.at[ys[j], n], ey_rs.at[ys[j], n])
            total = total + e_recv[ys[j], n].astype(F32)
        total = total.astype(BF16)
        if n < X - 1:
            e_sum[n] = total
            send(e_sum.at[n], e_p2.at[x], e2_ss.at[n], e2_rs.at[x], x_peers[n + 1])
        else:
            e_p2[x] = total

    def e_home(k):
        origin = xs[k]
        block = e_p2.at[origin]
        if k:
            arrived(block, e2_rs.at[origin])

        @pl.when(origin == y)
        def _():
            e_fin[y] = block[...]

        @pl.when(origin != y)
        def _():
            pltpu.make_async_remote_copy(
                src_ref=block, dst_ref=e_fin.at[y], send_sem=e1_ss.at[k], recv_sem=e1_rs.at[y],
                device_id=device(x, origin, z, c), device_id_type=pl.DeviceIdType.MESH,
            ).start()

    e_out(0)
    term = d_term(x)
    d_own[...] = term
    total = d_sums(term, x)
    for k in range(1, X):
        arrived(sx_recv.at[xs[k]], sx_rs.at[xs[k]])
        total = total + sx_recv[xs[k]]
    stats[1, t] = total
    send_stats(1)
    for way in (0, 1):
        value = merge_term(g_block(way, 1), half_rows(way))
        g_out(way, 1, way, value + g_in(way, 0, way))
    e_out(1)
    e_out(2)
    e_out(3)
    e_sum_up(0)
    g_step(2)

    means = totals(1)
    d_mean = spread(first, means)
    dn_mean = spread(second, means)
    dnormed = d_own[...]
    for k in (3, 1, 2):
        arrived(d_recv_buf.at[xs[k]], d_rs.at[xs[k]])
        dnormed = dnormed + d_recv_buf[xs[k]].astype(F32)
    grad_input = (dnormed - d_mean - normed_s[0] * dn_mean) * normed_s[1]
    for q in range(4):
        part = grad_input[:, q * FS:(q + 1) * FS]
        part = jnp.concatenate([part, jnp.zeros((G, 256 - FS), F32)], axis=1)
        rows = pl.ds(q, G, stride=4)
        proj_s[0, rows, :] = part[:, :128]
        proj_s[1, rows, :] = part[:, 128:]
    grad_rows = jnp.concatenate([proj_s[0], proj_s[1]], axis=1)
    grad_rows = jnp.transpose(grad_rows)[:FS].astype(BF16)

    for chunk in (0, 1):
        low, high = 640 * chunk, min(640 * (chunk + 1), PD)
        if chunk:
            t_s[chunk, :, 512:] = jnp.zeros((FS, 128), BF16)
        t_s[chunk, :, :high - low] = dot(
            grad_rows, patches_ref[low:high], ((1,), (1,))).astype(BF16)
        for p in range(50):
            i, j = p % 10, p // 10
            a_own[chunk, p // 13, p % 13] = t_s[chunk, 16 * i:16 * (i + 1), 128 * j:128 * (j + 1)]
        for p in range(50, 52):
            a_own[chunk, p // 13, p % 13] = jnp.zeros((16, 128), BF16)
        for k in (1, 3, 2):
            send(a_own.at[chunk, xs[k]], a_xr.at[chunk, x], ax_ss.at[chunk, k],
                 ax_rs.at[chunk, x], x_peers[k])

    def over_z(chunk):
        total = a_own[chunk, x].astype(F32)
        for k in (3, 1, 2):
            arrived(a_xr.at[chunk, xs[k]], ax_rs.at[chunk, xs[k]])
            total = total + a_xr[chunk, xs[k]].astype(F32)
        a_x[chunk, pl.ds(0, 13)] = total.astype(BF16)
        a_x[chunk, pl.ds(13, 3)] = jnp.zeros((3, 16, 128), BF16)
        for k in (1, 7, 2, 6, 3, 5, 4):
            send(a_x.at[chunk, pl.ds(2 * zs[k], 2)], a_zr.at[chunk, z], az_ss.at[chunk, k],
                 az_rs.at[chunk, z], z_peers[k])

    def back_over_z(chunk):
        total = a_x[chunk, pl.ds(2 * z, 2)].astype(F32)
        for k in range(1, Z):
            arrived(a_zr.at[chunk, zs[k]], az_rs.at[chunk, zs[k]])
            total = total + a_zr[chunk, zs[k]].astype(F32)
        mine = a_all.at[chunk, x, pl.ds(2 * z, 2)]
        mine[...] = total.astype(BF16)
        for k in (1, 7, 2, 6, 3, 5, 4):
            send(mine, mine, bz_ss.at[chunk, k], bz_rs.at[chunk, z], z_peers[k])

    def back_over_x(chunk):
        for k in range(1, Z):
            arrived(a_all.at[chunk, x, pl.ds(2 * zs[k], 2)], bz_rs.at[chunk, zs[k]])
        mine = a_all.at[chunk, x, pl.ds(0, 13)]
        for k in (1, 3, 2):
            send(mine, mine, bx_ss.at[chunk, k], bx_rs.at[chunk, x], x_peers[k])

    e_sum_up(1)
    g_step(3)
    over_z(0)
    over_z(1)
    e_sum_up(2)
    back_over_z(0)
    back_over_z(1)
    e_sum_up(3)
    back_over_x(0)
    back_over_x(1)
    e_home(3)
    e_home(2)
    e_home(1)
    e_home(0)

    term = merge_term(z)
    for half in (0, 1):
        gm_ref[pl.ds(half * HALF, HALF)] = (
            term[half_rows(half)] + g_in(0, 3, half) + g_in(1, 3, half))
    outputs = [pltpu.make_async_copy(gm_ref, gm_hbm, out_s.at[0])]
    outputs[0].start()

    for k in range(1, Y):
        arrived(e_fin.at[ys[k]], e1_rs.at[ys[k]])
    for k in range(QUAD):
        block = e_fin[k]
        embeds_ref[:, k * NC:(k + 1) * NC] = jnp.where(live_rows, block, jnp.zeros_like(block))
    outputs.append(pltpu.make_async_copy(embeds_ref, embeds_hbm, out_s.at[1]))
    outputs[1].start()

    for chunk in (0, 1):
        for k in range(1, X):
            arrived(a_all.at[chunk, xs[k], pl.ds(0, 13)], bx_rs.at[chunk, xs[k]])
        for p in range(50):
            i, j = p % 10, 5 * chunk + p // 10
            rows = slice(16 * i, 16 * (i + 1))
            tile = a_all[chunk, p // 13, p % 13].astype(F32)
            if j < 9:
                gp_ref[rows, 128 * j:128 * (j + 1)] = tile
            else:
                gp_ref[rows, 1152:] = tile[:, :PD - 1152]
    outputs.append(pltpu.make_async_copy(gp_ref, gp_hbm, out_s.at[2]))
    outputs[2].start()

    for k in range(X):
        @pl.when(xs[k] != y)
        def _():
            pltpu.make_async_remote_copy(
                src_ref=e_p2.at[xs[k]], dst_ref=e_fin.at[y], send_sem=e1_ss.at[k],
                recv_sem=e1_rs.at[y], device_id=device(x, xs[k], z, c),
                device_id_type=pl.DeviceIdType.MESH,
            ).wait_send()
    for copy in outputs:
        copy.wait()
    for copy in started:
        copy.wait_send()


def finish(embeds_in, gm_in, gp_in, embeds_out, gm_out, gp_out, sems):
    copies = []
    for i, (src, dst, rows) in enumerate(
        ((embeds_in, embeds_out, G), (gm_in, gm_out, K), (gp_in, gp_out, FS))
    ):
        for half in (0, 1):
            part = pl.ds(half * rows // 2, rows // 2)
            copies.append(pltpu.make_async_copy(src.at[part], dst.at[part], sems.at[i, half]))
    for copy in copies:
        copy.start()
    for copy in copies:
        copy.wait()


def body(patches, rank_groups, patch_weight, merge_weight, emb_grad):
    dma = pltpu.SemaphoreType.DMA
    rows = 4 * G
    scratch = [
        pltpu.VMEM((G, QUAD * NC), BF16),
        pltpu.VMEM((K, NC), F32),
        pltpu.VMEM((FS, PD), F32),
        pltpu.VMEM((PD, rows), BF16),
        pltpu.VMEM((FS, PD), BF16),
        pltpu.VMEM((G, QUAD * NC), BF16),
        pltpu.VMEM((Z, K, NC), BF16),
        pltpu.VMEM((QUAD, G, NC), BF16),
        pltpu.VMEM((Y, G, NC), BF16),
        pltpu.VMEM((X, Z, G, NC), BF16),
        pltpu.VMEM((X, G, K), BF16),
        pltpu.VMEM((K, X * G), BF16),
        pltpu.VMEM((2, rows, 128), F32),
        pltpu.VMEM((2, G, K), F32),
        pltpu.VMEM((2, T, 8, G), F32),
        pltpu.VMEM((X, 8, G), F32),
        pltpu.VMEM((X, 8, G), F32),
        pltpu.VMEM((2, 4, 2, HALF, NC), BF16),
        pltpu.VMEM((2, 4, 2, HALF, NC), BF16),
        pltpu.VMEM((X, G, K), BF16),
        pltpu.VMEM((G, K), F32),
        pltpu.VMEM((X, G, K), BF16),
        pltpu.VMEM((X, QUAD, G, NC), BF16),
        pltpu.VMEM((X, QUAD, G, NC), BF16),
        pltpu.VMEM((X, QUAD, G, NC), BF16),
        pltpu.VMEM((Y, X, G, NC), BF16),
        pltpu.VMEM((X, G, NC), BF16),
        pltpu.VMEM((X, G, NC), BF16),
        pltpu.VMEM((QUAD, G, NC), BF16),
        pltpu.VMEM((2, FS, 640), BF16),
        pltpu.VMEM((2, X, 13, 16, 128), BF16),
        pltpu.VMEM((2, X, 13, 16, 128), BF16),
        pltpu.VMEM((2, 16, 16, 128), BF16),
        pltpu.VMEM((2, Z, 2, 16, 128), BF16),
        pltpu.VMEM((2, X, 16, 16, 128), BF16),
        dma((4,)),
        dma((3,)),
    ]
    for shape in (
        (2, 4, 2), (4,), (4,), (4, 4), (4, 2), (4, 4), (2, 8), (4,), (4,),
        (4,), (2, 4, 2), (4,), (4, 4), (4,), (4,), (2, 4), (2, 8), (2, 8), (2, 4),
    ):
        scratch += [dma(shape), dma(shape)]
    results = (
        jax.ShapeDtypeStruct((G, QUAD * NC), BF16),
        jax.ShapeDtypeStruct((K, NC), F32),
        jax.ShapeDtypeStruct((FS, PD), F32),
    )
    hbm = pl.BlockSpec(memory_space=pl.ANY)
    partial = pl.pallas_call(
        kernel,
        out_shape=results,
        in_specs=[pl.BlockSpec(memory_space=pltpu.SMEM)] + [hbm] * 4,
        out_specs=(hbm, hbm, hbm),
        scratch_shapes=scratch,
        compiler_params=pltpu.CompilerParams(
            collective_id=0, has_side_effects=True, vmem_limit_bytes=56 * 2**20
        ),
        name="tower",
    )(rank_groups, patches.T, patch_weight.T, merge_weight.reshape(K, NC), emb_grad)
    embeds, grad_merge, grad_patch = pl.pallas_call(
        finish,
        out_shape=results,
        in_specs=[hbm, hbm, hbm],
        out_specs=(hbm, hbm, hbm),
        scratch_shapes=[dma((3, 2))],
        name="finish",
    )(*partial)
    return embeds, grad_merge.reshape(4, FS, NC), grad_patch.T


def solution(mesh):
    return jax.shard_map(
        body,
        mesh=mesh,
        in_specs=(
            P("dp", None),
            P("dp"),
            P(None, "tensor"),
            P(None, "tensor", "dp"),
            P("dp", "tensor"),
        ),
        out_specs=(P("dp", "tensor"), P(None, "tensor", "dp"), P(None, "tensor")),
        check_vma=False,
    )
```

time: 117 us -> 169 us (1.44); the launches traced: 117 us -> 166 us
  Pallas kernels: 111 us -> 165 us
  local copies, waits for them, and re-layouts: 4.82 us -> 0 us
    pallas_call x1 -> x2, Pallas kernels: 111 us -> 165 us  [the longest x1 103 us: body(): pl.pallas_call(kernel, out_shape=results, in_specs=[pl.BlockSpec(memory_s...]
    unnamed x5 -> x0, local copies, waits for them, and re-layouts: 4.82 us -> none
where the time goes in v3:
time: 169 us; the launch traced here: 166 us
  Pallas kernels  165 us (98%)
    pallas_call x1, Pallas kernels, body(): pl.pallas_call(kernel, out_shape=results, in_specs=[pl.BlockSpec(memory_s...  103 us
    pallas_call x1, Pallas kernels, body(): pl.pallas_call(finish, out_shape=results, in_specs=[hbm, hbm, hbm], out_s...  61.7 us

profile of v3, /device:TPU:1, one launch (start us, length us, event | category | flops | bytes accessed | tf_op | source)
XLA Modules:
  0.0 166.4 jit_solution(6715530605709807505)
XLA Ops:
  1.3 103.3 %tower.1 = (bf16[256,1024]{1,0:T(8,128)(2,1)}, f32[640,256]{1,0:T(8,128)}, f32[160,1176]{1,0:T(8,128)}) custom-call(s32[1]{0:T(128)S(6)} %copy.8.live_ref, bf16[1176,1024]{1,0:T(8,128)(2,1)} %bitcast.5, bf16[160,1176]{1,0:T(8,128)(2,1)} %bitcast.6, bf16[640,256]{1,0:T(8,128)(2,1)} %bitcast.7, bf16[256,1024]{1,0:T(8,128)(2,1)} %emb_hbm.1), custom_call_target="tpu_custom_call" | custom-call | tf_op jit(solution)/shard_map/tower/pallas_call | solution.py:564
  104.5 61.7 %finish.1 = (bf16[256,1024]{1,0:T(8,128)(2,1)}, f32[640,256]{1,0:T(8,128)}, f32[160,1176]{1,0:T(8,128)}) custom-call(bf16[256,1024]{1,0:T(8,128)(2,1)} %get-tuple-element.9.embeds_in, f32[640,256]{1,0:T(8,128)} %get-tuple-element.10.gm_in, f32[160,1176]{1,0:T(8,128)} %get-tuple-element.11.gp_in), custom_call_target="tpu_custom_call" | custom-call | tf_op jit(solution)/shard_map/finish/pallas_call | solution.py:575

commit v4 on v3

--- a/solution.py
+++ b/solution.py
@@ -240,57 +240,25 @@
         send(merged_all.at[x], merged_all.at[x], m_ss.at[k], m_rs.at[x], x_peers[k])
 
     w_fwd(2, 0)
+    cot_on(0)
     cot_out(1)
     cot_out(3)
+    w_fwd(2, 1)
     cot_out(2)
-    cot_on(0)
-    w_fwd(2, 1)
     merged_t[:, pl.ds(x * G, G)] = jnp.transpose(merged_all[x])
     cot_far(0)
+    w_fwd(3, 0)
     cot_on(1)
-    w_fwd(3, 0)
     cot_on(3)
     cot_far(1)
     cot_on(2)
     cot_far(3)
-    for k in range(1, X):
-        arrived(merged_all.at[xs[k]], m_rs.at[xs[k]])
-        merged_t[:, pl.ds(xs[k] * G, G)] = jnp.transpose(merged_all[xs[k]])
     cot_far(2)
+    w_finish()
     for k in (0, 1, 3, 2):
         cot_in(k)
-
-    def merge_term(block, rows=slice(None)):
-        return dot(merged_t[rows], cot_all[:, block].reshape(X * G, NC))
-
-    def g_block(way, step):
-        return wrap(z + 4 - step, Z) if way == 0 else wrap(z - 4 + step, Z)
-
-    def g_out(way, step, half, value):
-        g_send_buf[way, step, half] = value.astype(BF16)
-        send(g_send_buf.at[way, step, half], g_recv_buf.at[way, step, half],
-             g_ss.at[way, step, half], g_rs.at[way, step, half], right if way == 0 else left)
-
-    def g_in(way, step, half):
-        arrived(g_recv_buf.at[way, step, half], g_rs.at[way, step, half])
-        return g_recv_buf[way, step, half].astype(F32)
-
-    def half_rows(half):
-        return slice(half * HALF, (half + 1) * HALF)
-
-    for way in (0, 1):
-        g_out(way, 0, way, merge_term(g_block(way, 0), half_rows(way)))
-    for way in (0, 1):
-        g_out(way, 1, 1 - way, merge_term(g_block(way, 1), half_rows(1 - way)))
-
-    def g_step(step):
-        terms = [merge_term(g_block(way, step)) for way in (0, 1)]
-        for piece in (0, 1):
-            for way in (0, 1):
-                half = 1 - way if piece == 0 else way
-                g_out(way, step, half, terms[way][half_rows(half)] + g_in(way, step - 1, half))
-
-    w_finish()
+    for k in (3, 1, 2):
+        arrived(merged_all.at[xs[k]], m_rs.at[xs[k]])
 
     def d_term(owner):
         total = None
@@ -310,8 +278,39 @@
         d_send_buf[k] = term.astype(BF16)
         sx_send[k] = d_sums(term, xs[k])
         send(sx_send.at[k], sx_recv.at[x], sx_ss.at[k], sx_rs.at[x], x_peers[k])
-    for k in (1, 3, 2):
         send(d_send_buf.at[k], d_recv_buf.at[x], d_ss.at[k], d_rs.at[x], x_peers[k])
+
+    for k in range(1, X):
+        merged_t[:, pl.ds(xs[k] * G, G)] = jnp.transpose(merged_all[xs[k]])
+
+    def merge_term(block, rows=slice(None)):
+        return dot(merged_t[rows], cot_all[:, block].reshape(X * G, NC))
+
+    def g_block(way, step):
+        return wrap(z + 4 - step, Z) if way == 0 else wrap(z - 4 + step, Z)
+
+    def g_out(way, step, half, value):
+        g_send_buf[way, step, half] = value.astype(BF16)
+        send(g_send_buf.at[way, step, half], g_recv_buf.at[way, step, half],
+             g_ss.at[way, step, half], g_rs.at[way, step, half], right if way == 0 else left)
+
+    def g_in(way, step, half):
+        arrived(g_recv_buf.at[way, step, half], g_rs.at[way, step, half])
+        return g_recv_buf[way, step, half].astype(F32)
+
+    def half_rows(half):
+        return slice(half * HALF, (half + 1) * HALF)
+
+    for way in (0, 1):
+        g_out(way, 0, way, merge_term(g_block(way, 0), half_rows(way)))
+    for way in (0, 1):
+        g_out(way, 1, 1 - way, merge_term(g_block(way, 1), half_rows(1 - way)))
+
+    def g_piece(step, piece):
+        for way in (0, 1):
+            half = 1 - way if piece == 0 else way
+            term = merge_term(g_block(way, step), half_rows(half))
+            g_out(way, step, half, term + g_in(way, step - 1, half))
 
     for n in range(X):
         rows = merged_all[xs[(n + 1) % X]]
@@ -362,19 +361,18 @@
     term = d_term(x)
     d_own[...] = term
     total = d_sums(term, x)
+    g_piece(1, 1)
     for k in range(1, X):
         arrived(sx_recv.at[xs[k]], sx_rs.at[xs[k]])
         total = total + sx_recv[xs[k]]
     stats[1, t] = total
     send_stats(1)
-    for way in (0, 1):
-        value = merge_term(g_block(way, 1), half_rows(way))
-        g_out(way, 1, way, value + g_in(way, 0, way))
+    g_piece(2, 0)
     e_out(1)
     e_out(2)
     e_out(3)
+    g_piece(2, 1)
     e_sum_up(0)
-    g_step(2)
 
     means = totals(1)
     d_mean = spread(first, means)
@@ -393,6 +391,8 @@
     grad_rows = jnp.concatenate([proj_s[0], proj_s[1]], axis=1)
     grad_rows = jnp.transpose(grad_rows)[:FS].astype(BF16)
 
+    g_piece(3, 0)
+
     for chunk in (0, 1):
         low, high = 640 * chunk, min(640 * (chunk + 1), PD)
         if chunk:
@@ -436,8 +436,8 @@
         for k in (1, 3, 2):
             send(mine, mine, bx_ss.at[chunk, k], bx_rs.at[chunk, x], x_peers[k])
 
+    g_piece(3, 1)
     e_sum_up(1)
-    g_step(3)
     over_z(0)
     over_z(1)
     e_sum_up(2)
@@ -445,9 +445,9 @@
     back_over_z(1)
     e_sum_up(3)
     back_over_x(0)
-    back_over_x(1)
     e_home(3)
     e_home(2)
+    back_over_x(1)
     e_home(1)
     e_home(0)
 
@@ -494,18 +494,24 @@
         copy.wait_send()
 
 
-def finish(embeds_in, gm_in, gp_in, embeds_out, gm_out, gp_out, sems):
-    copies = []
-    for i, (src, dst, rows) in enumerate(
-        ((embeds_in, embeds_out, G), (gm_in, gm_out, K), (gp_in, gp_out, FS))
-    ):
+def finish(embeds_in, gm_in, gp_in, embeds_out, gm_out, gp_out, embeds_s, gm_s, gp_s, sems):
+    parts = []
+    for i, (src, held, dst, rows) in enumerate((
+        (embeds_in, embeds_s, embeds_out, G), (gm_in, gm_s, gm_out, K), (gp_in, gp_s, gp_out, FS)
+    )):
         for half in (0, 1):
             part = pl.ds(half * rows // 2, rows // 2)
-            copies.append(pltpu.make_async_copy(src.at[part], dst.at[part], sems.at[i, half]))
-    for copy in copies:
-        copy.start()
-    for copy in copies:
-        copy.wait()
+            parts.append((
+                pltpu.make_async_copy(src.at[part], held.at[part], sems.at[0, i, half]),
+                pltpu.make_async_copy(held.at[part], dst.at[part], sems.at[1, i, half]),
+            ))
+    for load, _ in parts:
+        load.start()
+    for load, store in parts:
+        load.wait()
+        store.start()
+    for _, store in parts:
+        store.wait()
 
 
 def body(patches, rank_groups, patch_weight, merge_weight, emb_grad):
@@ -577,7 +583,12 @@
         out_shape=results,
         in_specs=[hbm, hbm, hbm],
         out_specs=(hbm, hbm, hbm),
-        scratch_shapes=[dma((3, 2))],
+        scratch_shapes=[
+            pltpu.VMEM((G, QUAD * NC), BF16),
+            pltpu.VMEM((K, NC), F32),
+            pltpu.VMEM((FS, PD), F32),
+            dma((2, 3, 2)),
+        ],
         name="finish",
     )(*partial)
     return embeds, grad_merge.reshape(4, FS, NC), grad_patch.T

time: 169 us -> 103 us (0.61); the launches traced: 166 us -> 103 us
  Pallas kernels: 165 us -> 102 us
    pallas_call x1, Pallas kernels: 61.7 us -> 2.35 us  [body(): pl.pallas_call(finish, out_shape=results, in_specs=[hbm, hbm, hbm], out_s...]
    pallas_call x1, Pallas kernels: 103 us -> 99.2 us  [body(): pl.pallas_call(kernel, out_shape=results, in_specs=[pl.BlockSpec(memory_s...]
where the time goes in v4:
time: 103 us
  Pallas kernels  102 us (99%)
  between operations  1.44 us (1%)
    pallas_call x1, Pallas kernels, body(): pl.pallas_call(kernel, out_shape=results, in_specs=[pl.BlockSpec(memory_s...  99.2 us
    pallas_call x1, Pallas kernels, body(): pl.pallas_call(finish, out_shape=results, in_specs=[hbm, hbm, hbm], out_s...  2.35 us

profile of v4, /device:TPU:1, one launch (start us, length us, event | category | flops | bytes accessed | tf_op | source)
XLA Modules:
  0.0 103.0 jit_solution(1042277190054093585)
XLA Ops:
  1.3 99.2 %tower.1 = (bf16[256,1024]{1,0:T(8,128)(2,1)}, f32[640,256]{1,0:T(8,128)}, f32[160,1176]{1,0:T(8,128)}) custom-call(s32[1]{0:T(128)S(6)} %copy.8.live_ref, bf16[1176,1024]{1,0:T(8,128)(2,1)} %bitcast.5, bf16[160,1176]{1,0:T(8,128)(2,1)} %bitcast.6, bf16[640,256]{1,0:T(8,128)(2,1)} %bitcast.7, bf16[256,1024]{1,0:T(8,128)(2,1)} %emb_hbm.1), custom_call_target="tpu_custom_call" | custom-call | tf_op jit(solution)/shard_map/tower/pallas_call | solution.py:570
  100.5 2.4 %finish.1 = (bf16[256,1024]{1,0:T(8,128)(2,1)}, f32[640,256]{1,0:T(8,128)}, f32[160,1176]{1,0:T(8,128)}) custom-call(bf16[256,1024]{1,0:T(8,128)(2,1)} %get-tuple-element.9.embeds_in, f32[640,256]{1,0:T(8,128)} %get-tuple-element.10.gm_in, f32[160,1176]{1,0:T(8,128)} %get-tuple-element.11.gp_in), custom_call_target="tpu_custom_call" | custom-call | tf_op jit(solution)/shard_map/finish/pallas_call | solution.py:581

commit v5 on v4

--- a/solution.py
+++ b/solution.py
@@ -43,13 +43,14 @@
     embeds_ref, gm_ref, gp_ref,
     patches_ref, pw_ref, emb_ref,
     wg, cot_own, cot_p1, cot_all, merged_all, merged_t, proj_s, normed_s,
-    stats, sx_send, sx_recv, g_send_buf, g_recv_buf, d_send_buf, d_own, d_recv_buf,
+    stats, sx_send, sx_recv, g_send_buf, g_recv_buf,
+    d_send_buf, d_keep, d_far, d_own, d_recv_buf,
     e_sib_send, e_sib_recv, e_send, e_recv, e_sum, e_p2, e_fin,
     t_s, a_own, a_xr, a_x, a_zr, a_all,
     in_s, out_s,
     w_ss, w_rs, p1_ss, p1_rs, p2_ss, p2_rs, p3_ss, p3_rs, ph_ss, ph_rs, cs_ss, cs_rs,
     st_ss, st_rs, sx_ss, sx_rs, m_ss, m_rs,
-    d_ss, d_rs, g_ss, g_rs, es_ss, es_rs, ey_ss, ey_rs, e2_ss, e2_rs, e1_ss, e1_rs,
+    d_ss, d_rs, df_ss, df_rs, g_ss, g_rs, es_ss, es_rs, ey_ss, ey_rs, e2_ss, e2_rs, e1_ss, e1_rs,
     ax_ss, ax_rs, az_ss, az_rs, bz_ss, bz_rs, bx_ss, bx_rs,
 ):
     dp = lax.axis_index("dp")
@@ -111,8 +112,13 @@
 
     pl.semaphore_wait(barrier, len(greeted))
 
-    for k in range(1, Y):
-        send(cot_own.at[ys[k]], cot_p1.at[y], p1_ss.at[k], p1_rs.at[y], y_peers[k])
+    def rows_of(half):
+        return pl.ds(half * 128, 128)
+
+    for half in (0, 1):
+        for k in (1, 3, 2):
+            send(cot_own.at[ys[k], rows_of(half)], cot_p1.at[y, rows_of(half)],
+                 p1_ss.at[k, half], p1_rs.at[y, half], y_peers[k])
 
     def w_part(index, half):
         return wg.at[index, pl.ds(half * HALF, HALF)]
@@ -174,21 +180,20 @@
         + dot(second, projected * projected, ((1,), (1,)), HIGH)
     )
     send_stats(0)
-    w_fwd(1, 0)
-
-    for k in (1, 3, 2, 0):
-        origin = xs[k]
-        block = cot_p1.at[origin]
-
-        @pl.when(origin != y)
-        def _():
-            arrived(block, p1_rs.at[origin])
-
-        slot = cot_all.at[x, c * QUAD + y]
-        if k:
-            send(block, slot, p2_ss.at[k], p2_rs.at[x], x_peers[k])
-        else:
-            slot[...] = block[...]
+    def cot_over_x(half):
+        for k in (1, 3, 2, 0):
+            origin = xs[k]
+            block = cot_p1.at[origin, rows_of(half)]
+
+            @pl.when(origin != y)
+            def _():
+                arrived(block, p1_rs.at[origin, half])
+
+            slot = cot_all.at[x, c * QUAD + y, rows_of(half)]
+            if k:
+                send(block, slot, p2_ss.at[k, half], p2_rs.at[x, half], x_peers[k])
+            else:
+                slot[...] = block[...]
 
     def cot_block(k, j):
         return cot_all.at[xs[k], c * QUAD + ys[j]]
@@ -197,33 +202,40 @@
         block = cot_block(k, j)
         send(block, block, cs_ss.at[k, j], cs_rs.at[xs[k], ys[j]], sibling)
 
-    def cot_out(k):
-        block = cot_block(k, 0)
+    def cot_out(k, half):
+        part = cot_block(k, 0).at[rows_of(half)]
         if k:
-            arrived(block, p2_rs.at[xs[k]])
+            arrived(part, p2_rs.at[xs[k], half])
         for j in (1, 3):
-            send(block, block, p3_ss.at[k, j], p3_rs.at[xs[k], y], y_peers[j])
-        to_sibling(k, 0)
+            send(part, part, p3_ss.at[k, j, half], p3_rs.at[xs[k], y, half], y_peers[j])
+        if half:
+            to_sibling(k, 0)
 
     def cot_on(k):
         for half, j in ((0, 1), (1, 3)):
-            block = cot_block(k, j)
-            arrived(block, p3_rs.at[xs[k], ys[j]])
-            part = block.at[pl.ds(half * 128, 128)]
+            part = cot_block(k, j).at[rows_of(half)]
+            arrived(part, p3_rs.at[xs[k], ys[j], half])
             send(part, part, ph_ss.at[k, half], ph_rs.at[xs[k], half], y_peers[4 - j])
-        to_sibling(k, 1)
-        to_sibling(k, 3)
+        for half, j in ((1, 1), (0, 3)):
+            arrived(cot_block(k, j).at[rows_of(half)], p3_rs.at[xs[k], ys[j], half])
+            to_sibling(k, j)
 
     def cot_far(k):
         for half in (0, 1):
-            arrived(cot_block(k, 2).at[pl.ds(half * 128, 128)], ph_rs.at[xs[k], half])
+            arrived(cot_block(k, 2).at[rows_of(half)], ph_rs.at[xs[k], half])
         to_sibling(k, 2)
 
     def cot_in(k):
         for j in range(Y):
             arrived(cot_all.at[xs[k], (1 - c) * QUAD + ys[j]], cs_rs.at[xs[k], ys[j]])
 
-    cot_out(0)
+    cot_over_x(0)
+    w_fwd(1, 0)
+    cot_out(0, 0)
+    cot_over_x(1)
+    cot_out(0, 1)
+    cot_out(1, 0)
+    cot_out(3, 0)
     w_fwd(1, 1)
 
     means = totals(0)
@@ -239,12 +251,13 @@
     for k in range(1, X):
         send(merged_all.at[x], merged_all.at[x], m_ss.at[k], m_rs.at[x], x_peers[k])
 
+    cot_out(2, 0)
+    cot_out(1, 1)
+    cot_out(3, 1)
     w_fwd(2, 0)
     cot_on(0)
-    cot_out(1)
-    cot_out(3)
+    cot_out(2, 1)
     w_fwd(2, 1)
-    cot_out(2)
     merged_t[:, pl.ds(x * G, G)] = jnp.transpose(merged_all[x])
     cot_far(0)
     w_fwd(3, 0)
@@ -273,12 +286,31 @@
         return (dot(first.astype(BF16), rounded, ((1,), (1,)))
                 + dot(second.astype(BF16), product, ((1,), (1,))))
 
-    for k in (1, 3, 2):
+    def d_near(way, half, to):
+        slot = 1 if way == 0 else 3
+        part = pl.ds(half * 128, 128)
+        send(d_send_buf.at[slot, part], d_recv_buf.at[way, part], d_ss.at[way, half],
+             d_rs.at[way, half], to)
+
+    for k, to in ((2, None), (1, x_peers[1]), (3, x_peers[3])):
         term = d_term(xs[k])
         d_send_buf[k] = term.astype(BF16)
         sx_send[k] = d_sums(term, xs[k])
         send(sx_send.at[k], sx_recv.at[x], sx_ss.at[k], sx_rs.at[x], x_peers[k])
-        send(d_send_buf.at[k], d_recv_buf.at[x], d_ss.at[k], d_rs.at[x], x_peers[k])
+        if k == 2:
+            for way, peer in ((0, x_peers[1]), (1, x_peers[3])):
+                send(d_send_buf.at[2, rows_of(way)], d_far.at[way], df_ss.at[way],
+                     df_rs.at[way], peer)
+        else:
+            way = 0 if k == 1 else 1
+            d_keep[way] = term[way * 128:(way + 1) * 128]
+            d_near(way, 1 - way, to)
+
+    def d_combine():
+        for way, slot, to in ((0, 1, x_peers[1]), (1, 3, x_peers[3])):
+            arrived(d_far.at[way], df_rs.at[way])
+            d_send_buf[slot, rows_of(way)] = (d_keep[way] + d_far[way].astype(F32)).astype(BF16)
+            d_near(way, way, to)
 
     for k in range(1, X):
         merged_t[:, pl.ds(xs[k] * G, G)] = jnp.transpose(merged_all[xs[k]])
@@ -357,30 +389,30 @@
                 device_id=device(x, origin, z, c), device_id_type=pl.DeviceIdType.MESH,
             ).start()
 
-    e_out(0)
+    d_combine()
     term = d_term(x)
     d_own[...] = term
     total = d_sums(term, x)
-    g_piece(1, 1)
     for k in range(1, X):
         arrived(sx_recv.at[xs[k]], sx_rs.at[xs[k]])
         total = total + sx_recv[xs[k]]
     stats[1, t] = total
     send_stats(1)
-    g_piece(2, 0)
+    e_out(0)
+    g_piece(1, 1)
     e_out(1)
     e_out(2)
     e_out(3)
-    g_piece(2, 1)
-    e_sum_up(0)
+    g_piece(2, 0)
 
     means = totals(1)
     d_mean = spread(first, means)
     dn_mean = spread(second, means)
     dnormed = d_own[...]
-    for k in (3, 1, 2):
-        arrived(d_recv_buf.at[xs[k]], d_rs.at[xs[k]])
-        dnormed = dnormed + d_recv_buf[xs[k]].astype(F32)
+    for way in (0, 1):
+        for half in (1 - way, way):
+            arrived(d_recv_buf.at[way, rows_of(half)], d_rs.at[way, half])
+        dnormed = dnormed + d_recv_buf[way].astype(F32)
     grad_input = (dnormed - d_mean - normed_s[0] * dn_mean) * normed_s[1]
     for q in range(4):
         part = grad_input[:, q * FS:(q + 1) * FS]
@@ -390,8 +422,6 @@
         proj_s[1, rows, :] = part[:, 128:]
     grad_rows = jnp.concatenate([proj_s[0], proj_s[1]], axis=1)
     grad_rows = jnp.transpose(grad_rows)[:FS].astype(BF16)
-
-    g_piece(3, 0)
 
     for chunk in (0, 1):
         low, high = 640 * chunk, min(640 * (chunk + 1), PD)
@@ -436,27 +466,34 @@
         for k in (1, 3, 2):
             send(mine, mine, bx_ss.at[chunk, k], bx_rs.at[chunk, x], x_peers[k])
 
+    outputs = []
+
+    def g_finish():
+        term = merge_term(z)
+        for half in (0, 1):
+            gm_ref[pl.ds(half * HALF, HALF)] = (
+                term[half_rows(half)] + g_in(0, 3, half) + g_in(1, 3, half))
+        outputs.append(pltpu.make_async_copy(gm_ref, gm_hbm, out_s.at[0]))
+        outputs[0].start()
+
+    g_piece(2, 1)
+    e_sum_up(0)
+    g_piece(3, 0)
+    over_z(0)
     g_piece(3, 1)
+    over_z(1)
     e_sum_up(1)
-    over_z(0)
-    over_z(1)
-    e_sum_up(2)
+    e_home(3)
     back_over_z(0)
     back_over_z(1)
+    e_sum_up(2)
+    e_home(2)
+    g_finish()
+    back_over_x(0)
+    back_over_x(1)
     e_sum_up(3)
-    back_over_x(0)
-    e_home(3)
-    e_home(2)
-    back_over_x(1)
+    e_home(0)
     e_home(1)
-    e_home(0)
-
-    term = merge_term(z)
-    for half in (0, 1):
-        gm_ref[pl.ds(half * HALF, HALF)] = (
-            term[half_rows(half)] + g_in(0, 3, half) + g_in(1, 3, half))
-    outputs = [pltpu.make_async_copy(gm_ref, gm_hbm, out_s.at[0])]
-    outputs[0].start()
 
     for k in range(1, Y):
         arrived(e_fin.at[ys[k]], e1_rs.at[ys[k]])
@@ -538,8 +575,10 @@
         pltpu.VMEM((2, 4, 2, HALF, NC), BF16),
         pltpu.VMEM((2, 4, 2, HALF, NC), BF16),
         pltpu.VMEM((X, G, K), BF16),
+        pltpu.VMEM((2, 128, K), F32),
+        pltpu.VMEM((2, 128, K), BF16),
         pltpu.VMEM((G, K), F32),
-        pltpu.VMEM((X, G, K), BF16),
+        pltpu.VMEM((2, G, K), BF16),
         pltpu.VMEM((X, QUAD, G, NC), BF16),
         pltpu.VMEM((X, QUAD, G, NC), BF16),
         pltpu.VMEM((X, QUAD, G, NC), BF16),
@@ -557,8 +596,8 @@
         dma((3,)),
     ]
     for shape in (
-        (2, 4, 2), (4,), (4,), (4, 4), (4, 2), (4, 4), (2, 8), (4,), (4,),
-        (4,), (2, 4, 2), (4,), (4, 4), (4,), (4,), (2, 4), (2, 8), (2, 8), (2, 4),
+        (2, 4, 2), (4, 2), (4, 2), (4, 4, 2), (4, 2), (4, 4), (2, 8), (4,), (4,),
+        (2, 2), (2,), (2, 4, 2), (4,), (4, 4), (4,), (4,), (2, 4), (2, 8), (2, 8), (2, 4),
     ):
         scratch += [dma(shape), dma(shape)]
     results = (

time: 103 us -> 102 us (level)
  no operation moved by 1% of the time
where the time goes in v5:
time: 102 us
  Pallas kernels  101 us (99%)
  between operations  1.44 us (1%)
    pallas_call x1, Pallas kernels, body(): pl.pallas_call(kernel, out_shape=results, in_specs=[pl.BlockSpec(memory_s...  98.4 us
    pallas_call x1, Pallas kernels, body(): pl.pallas_call(finish, out_shape=results, in_specs=[hbm, hbm, hbm], out_s...  2.35 us

profile of v5, /device:TPU:1, one launch (start us, length us, event | category | flops | bytes accessed | tf_op | source)
XLA Modules:
  0.0 102.2 jit_solution(12898613334321193443)
XLA Ops:
  1.3 98.4 %tower.1 = (bf16[256,1024]{1,0:T(8,128)(2,1)}, f32[640,256]{1,0:T(8,128)}, f32[160,1176]{1,0:T(8,128)}) custom-call(s32[1]{0:T(128)S(6)} %copy.8.live_ref, bf16[1176,1024]{1,0:T(8,128)(2,1)} %bitcast.5, bf16[160,1176]{1,0:T(8,128)(2,1)} %bitcast.6, bf16[640,256]{1,0:T(8,128)(2,1)} %bitcast.7, bf16[256,1024]{1,0:T(8,128)(2,1)} %emb_hbm.1), custom_call_target="tpu_custom_call" | custom-call | tf_op jit(solution)/shard_map/tower/pallas_call | solution.py:609
  99.7 2.4 %finish.1 = (bf16[256,1024]{1,0:T(8,128)(2,1)}, f32[640,256]{1,0:T(8,128)}, f32[160,1176]{1,0:T(8,128)}) custom-call(bf16[256,1024]{1,0:T(8,128)(2,1)} %get-tuple-element.9.embeds_in, f32[640,256]{1,0:T(8,128)} %get-tuple-element.10.gm_in, f32[160,1176]{1,0:T(8,128)} %get-tuple-element.11.gp_in), custom_call_target="tpu_custom_call" | custom-call | tf_op jit(solution)/shard_map/finish/pallas_call | solution.py:620

commit v6 on v5

--- a/solution.py
+++ b/solution.py
@@ -45,12 +45,12 @@
     wg, cot_own, cot_p1, cot_all, merged_all, merged_t, proj_s, normed_s,
     stats, sx_send, sx_recv, g_send_buf, g_recv_buf,
     d_send_buf, d_keep, d_far, d_own, d_recv_buf,
-    e_sib_send, e_sib_recv, e_send, e_recv, e_sum, e_p2, e_fin,
+    e_sib_send, e_sib_recv, e_send, e_far, e_recv, e_sum, e_p2, e_fin,
     t_s, a_own, a_xr, a_x, a_zr, a_all,
     in_s, out_s,
     w_ss, w_rs, p1_ss, p1_rs, p2_ss, p2_rs, p3_ss, p3_rs, ph_ss, ph_rs, cs_ss, cs_rs,
     st_ss, st_rs, sx_ss, sx_rs, m_ss, m_rs,
-    d_ss, d_rs, df_ss, df_rs, g_ss, g_rs, es_ss, es_rs, ey_ss, ey_rs, e2_ss, e2_rs, e1_ss, e1_rs,
+    d_ss, d_rs, df_ss, df_rs, g_ss, g_rs, es_ss, es_rs, ef_ss, ef_rs, ey_ss, ey_rs, e2_ss, e2_rs, e1_ss, e1_rs,
     ax_ss, ax_rs, az_ss, az_rs, bz_ss, bz_rs, bx_ss, bx_rs,
 ):
     dp = lax.axis_index("dp")
@@ -266,12 +266,20 @@
     cot_far(1)
     cot_on(2)
     cot_far(3)
+    w_finish()
+    for k in (3, 1, 2):
+        arrived(merged_all.at[xs[k]], m_rs.at[xs[k]])
+
+    for n in range(X):
+        rows = merged_all[xs[(n + 1) % X]]
+        for m in range(QUAD):
+            block = wg[(1 - c) * QUAD + ys[(m + 1) % Y]]
+            e_sib_send[n, m] = dot(rows, block).astype(BF16)
+        send(e_sib_send.at[n], e_sib_recv.at[n], es_ss.at[n], es_rs.at[n], sibling)
+
     cot_far(2)
-    w_finish()
     for k in (0, 1, 3, 2):
         cot_in(k)
-    for k in (3, 1, 2):
-        arrived(merged_all.at[xs[k]], m_rs.at[xs[k]])
 
     def d_term(owner):
         total = None
@@ -312,59 +320,37 @@
             d_send_buf[slot, rows_of(way)] = (d_keep[way] + d_far[way].astype(F32)).astype(BF16)
             d_near(way, way, to)
 
-    for k in range(1, X):
-        merged_t[:, pl.ds(xs[k] * G, G)] = jnp.transpose(merged_all[xs[k]])
-
-    def merge_term(block, rows=slice(None)):
-        return dot(merged_t[rows], cot_all[:, block].reshape(X * G, NC))
-
-    def g_block(way, step):
-        return wrap(z + 4 - step, Z) if way == 0 else wrap(z - 4 + step, Z)
-
-    def g_out(way, step, half, value):
-        g_send_buf[way, step, half] = value.astype(BF16)
-        send(g_send_buf.at[way, step, half], g_recv_buf.at[way, step, half],
-             g_ss.at[way, step, half], g_rs.at[way, step, half], right if way == 0 else left)
-
-    def g_in(way, step, half):
-        arrived(g_recv_buf.at[way, step, half], g_rs.at[way, step, half])
-        return g_recv_buf[way, step, half].astype(F32)
-
-    def half_rows(half):
-        return slice(half * HALF, (half + 1) * HALF)
-
-    for way in (0, 1):
-        g_out(way, 0, way, merge_term(g_block(way, 0), half_rows(way)))
-    for way in (0, 1):
-        g_out(way, 1, 1 - way, merge_term(g_block(way, 1), half_rows(1 - way)))
-
-    def g_piece(step, piece):
-        for way in (0, 1):
-            half = 1 - way if piece == 0 else way
-            term = merge_term(g_block(way, step), half_rows(half))
-            g_out(way, step, half, term + g_in(way, step - 1, half))
-
-    for n in range(X):
-        rows = merged_all[xs[(n + 1) % X]]
-        for m in range(QUAD):
-            block = wg[(1 - c) * QUAD + ys[(m + 1) % Y]]
-            e_sib_send[n, m] = dot(rows, block).astype(BF16)
-        send(e_sib_send.at[n], e_sib_recv.at[n], es_ss.at[n], es_rs.at[n], sibling)
-
     def e_out(n):
         rows = merged_all[xs[(n + 1) % X]]
         arrived(e_sib_recv.at[n], es_rs.at[n])
-        for m in range(QUAD):
+        for m in (1, 0, 2, 3):
             value = dot(rows, wg[c * QUAD + ys[(m + 1) % Y]]) + e_sib_recv[n, m].astype(F32)
             e_send[n, m] = value.astype(BF16)
-            if m < QUAD - 1:
-                send(e_send.at[n, m], e_recv.at[y, n], ey_ss.at[n, m], ey_rs.at[y, n], y_peers[m + 1])
+            if m == 1:
+                for way, peer in ((0, y_peers[1]), (1, y_peers[3])):
+                    send(e_send.at[n, 1, rows_of(way)], e_far.at[n, way], ef_ss.at[n, way],
+                         ef_rs.at[n, way], peer)
+            elif m < QUAD - 1:
+                e_near(n, 0 if m == 0 else 1, 1 if m == 0 else 0)
+
+    def e_near(n, way, half):
+        slot, peer = (0, y_peers[1]) if way == 0 else (2, y_peers[3])
+        send(e_send.at[n, slot, rows_of(half)], e_recv.at[n, way, rows_of(half)],
+             ey_ss.at[n, way, half], ey_rs.at[n, way, half], peer)
+
+    def e_combine(n):
+        for way, slot in ((0, 0), (1, 2)):
+            arrived(e_far.at[n, way], ef_rs.at[n, way])
+            part = e_send.at[n, slot, rows_of(way)]
+            part[...] = (part[...].astype(F32) + e_far[n, way].astype(F32)).astype(BF16)
+            e_near(n, way, way)
 
     def e_sum_up(n):
         total = e_send[n, QUAD - 1].astype(F32)
-        for j in range(1, Y):
-            arrived(e_recv.at[ys[j], n], ey_rs.at[ys[j], n])
-            total = total + e_recv[ys[j], n].astype(F32)
+        for way in (0, 1):
+            for half in (1 - way, way):
+                arrived(e_recv.at[n, way, rows_of(half)], ey_rs.at[n, way, half])
+            total = total + e_recv[n, way].astype(F32)
         total = total.astype(BF16)
         if n < X - 1:
             e_sum[n] = total
@@ -388,6 +374,39 @@
                 src_ref=block, dst_ref=e_fin.at[y], send_sem=e1_ss.at[k], recv_sem=e1_rs.at[y],
                 device_id=device(x, origin, z, c), device_id_type=pl.DeviceIdType.MESH,
             ).start()
+
+    e_out(0)
+    for k in range(1, X):
+        merged_t[:, pl.ds(xs[k] * G, G)] = jnp.transpose(merged_all[xs[k]])
+
+    def merge_term(block, rows=slice(None)):
+        return dot(merged_t[rows], cot_all[:, block].reshape(X * G, NC))
+
+    def g_block(way, step):
+        return wrap(z + 4 - step, Z) if way == 0 else wrap(z - 4 + step, Z)
+
+    def g_out(way, step, half, value):
+        g_send_buf[way, step, half] = value.astype(BF16)
+        send(g_send_buf.at[way, step, half], g_recv_buf.at[way, step, half],
+             g_ss.at[way, step, half], g_rs.at[way, step, half], right if way == 0 else left)
+
+    def g_in(way, step, half):
+        arrived(g_recv_buf.at[way, step, half], g_rs.at[way, step, half])
+        return g_recv_buf[way, step, half].astype(F32)
+
+    def half_rows(half):
+        return slice(half * HALF, (half + 1) * HALF)
+
+    for way in (0, 1):
+        g_out(way, 0, way, merge_term(g_block(way, 0), half_rows(way)))
+    for way in (0, 1):
+        g_out(way, 1, 1 - way, merge_term(g_block(way, 1), half_rows(1 - way)))
+
+    def g_piece(step, piece):
+        for way in (0, 1):
+            half = 1 - way if piece == 0 else way
+            term = merge_term(g_block(way, step), half_rows(half))
+            g_out(way, step, half, term + g_in(way, step - 1, half))
 
     d_combine()
     term = d_term(x)
@@ -398,12 +417,14 @@
         total = total + sx_recv[xs[k]]
     stats[1, t] = total
     send_stats(1)
-    e_out(0)
+    e_combine(0)
+    e_out(1)
     g_piece(1, 1)
-    e_out(1)
     e_out(2)
     e_out(3)
+    e_combine(1)
     g_piece(2, 0)
+    e_combine(2)
 
     means = totals(1)
     d_mean = spread(first, means)
@@ -413,6 +434,7 @@
         for half in (1 - way, way):
             arrived(d_recv_buf.at[way, rows_of(half)], d_rs.at[way, half])
         dnormed = dnormed + d_recv_buf[way].astype(F32)
+    e_combine(3)
     grad_input = (dnormed - d_mean - normed_s[0] * dn_mean) * normed_s[1]
     for q in range(4):
         part = grad_input[:, q * FS:(q + 1) * FS]
@@ -479,21 +501,21 @@
     g_piece(2, 1)
     e_sum_up(0)
     g_piece(3, 0)
+    e_sum_up(1)
     over_z(0)
+    e_sum_up(2)
+    e_sum_up(3)
+    e_home(0)
+    over_z(1)
     g_piece(3, 1)
-    over_z(1)
-    e_sum_up(1)
     e_home(3)
+    e_home(2)
     back_over_z(0)
+    e_home(1)
     back_over_z(1)
-    e_sum_up(2)
-    e_home(2)
     g_finish()
     back_over_x(0)
     back_over_x(1)
-    e_sum_up(3)
-    e_home(0)
-    e_home(1)
 
     for k in range(1, Y):
         arrived(e_fin.at[ys[k]], e1_rs.at[ys[k]])
@@ -582,7 +604,8 @@
         pltpu.VMEM((X, QUAD, G, NC), BF16),
         pltpu.VMEM((X, QUAD, G, NC), BF16),
         pltpu.VMEM((X, QUAD, G, NC), BF16),
-        pltpu.VMEM((Y, X, G, NC), BF16),
+        pltpu.VMEM((X, 2, 128, NC), BF16),
+        pltpu.VMEM((X, 2, G, NC), BF16),
         pltpu.VMEM((X, G, NC), BF16),
         pltpu.VMEM((X, G, NC), BF16),
         pltpu.VMEM((QUAD, G, NC), BF16),
@@ -597,7 +620,7 @@
     ]
     for shape in (
         (2, 4, 2), (4, 2), (4, 2), (4, 4, 2), (4, 2), (4, 4), (2, 8), (4,), (4,),
-        (2, 2), (2,), (2, 4, 2), (4,), (4, 4), (4,), (4,), (2, 4), (2, 8), (2, 8), (2, 4),
+        (2, 2), (2,), (2, 4, 2), (4,), (4, 2), (4, 2, 2), (4,), (4,), (2, 4), (2, 8), (2, 8), (2, 4),
     ):
         scratch += [dma(shape), dma(shape)]
     results = (

time: 102 us -> 102 us (level)
  no operation moved by 1% of the time
where the time goes in v6:
time: 102 us; the launch traced here: 101 us
  Pallas kernels  100 us (98%)
  between operations  1.44 us (1%)
    pallas_call x1, Pallas kernels, body(): pl.pallas_call(kernel, out_shape=results, in_specs=[pl.BlockSpec(memory_s...  97.7 us
    pallas_call x1, Pallas kernels, body(): pl.pallas_call(finish, out_shape=results, in_specs=[hbm, hbm, hbm], out_s...  2.35 us

profile of v6, /device:TPU:1, one launch (start us, length us, event | category | flops | bytes accessed | tf_op | source)
XLA Modules:
  0.0 101.5 jit_solution(7278442736111092660)
XLA Ops:
  1.3 97.7 %tower.1 = (bf16[256,1024]{1,0:T(8,128)(2,1)}, f32[640,256]{1,0:T(8,128)}, f32[160,1176]{1,0:T(8,128)}) custom-call(s32[1]{0:T(128)S(6)} %copy.8.live_ref, bf16[1176,1024]{1,0:T(8,128)(2,1)} %bitcast.5, bf16[160,1176]{1,0:T(8,128)(2,1)} %bitcast.6, bf16[640,256]{1,0:T(8,128)(2,1)} %bitcast.7, bf16[256,1024]{1,0:T(8,128)(2,1)} %emb_hbm.1), custom_call_target="tpu_custom_call" | custom-call | tf_op jit(solution)/shard_map/tower/pallas_call | solution.py:632
  99.0 2.4 %finish.1 = (bf16[256,1024]{1,0:T(8,128)(2,1)}, f32[640,256]{1,0:T(8,128)}, f32[160,1176]{1,0:T(8,128)}) custom-call(bf16[256,1024]{1,0:T(8,128)(2,1)} %get-tuple-element.9.embeds_in, f32[640,256]{1,0:T(8,128)} %get-tuple-element.10.gm_in, f32[160,1176]{1,0:T(8,128)} %get-tuple-element.11.gp_in), custom_call_target="tpu_custom_call" | custom-call | tf_op jit(solution)/shard_map/finish/pallas_call | solution.py:643

commit v7 on v6

--- a/solution.py
+++ b/solution.py
@@ -300,7 +300,7 @@
         send(d_send_buf.at[slot, part], d_recv_buf.at[way, part], d_ss.at[way, half],
              d_rs.at[way, half], to)
 
-    for k, to in ((2, None), (1, x_peers[1]), (3, x_peers[3])):
+    def d_out(k):
         term = d_term(xs[k])
         d_send_buf[k] = term.astype(BF16)
         sx_send[k] = d_sums(term, xs[k])
@@ -312,7 +312,7 @@
         else:
             way = 0 if k == 1 else 1
             d_keep[way] = term[way * 128:(way + 1) * 128]
-            d_near(way, 1 - way, to)
+            d_near(way, 1 - way, x_peers[k])
 
     def d_combine():
         for way, slot, to in ((0, 1, x_peers[1]), (1, 3, x_peers[3])):
@@ -320,18 +320,23 @@
             d_send_buf[slot, rows_of(way)] = (d_keep[way] + d_far[way].astype(F32)).astype(BF16)
             d_near(way, way, to)
 
-    def e_out(n):
-        rows = merged_all[xs[(n + 1) % X]]
+    def e_term(n, m):
+        value = dot(merged_all[xs[(n + 1) % X]], wg[c * QUAD + ys[(m + 1) % Y]])
+        e_send[n, m] = (value + e_sib_recv[n, m].astype(F32)).astype(BF16)
+
+    def e_far_out(n):
         arrived(e_sib_recv.at[n], es_rs.at[n])
-        for m in (1, 0, 2, 3):
-            value = dot(rows, wg[c * QUAD + ys[(m + 1) % Y]]) + e_sib_recv[n, m].astype(F32)
-            e_send[n, m] = value.astype(BF16)
-            if m == 1:
-                for way, peer in ((0, y_peers[1]), (1, y_peers[3])):
-                    send(e_send.at[n, 1, rows_of(way)], e_far.at[n, way], ef_ss.at[n, way],
-                         ef_rs.at[n, way], peer)
-            elif m < QUAD - 1:
-                e_near(n, 0 if m == 0 else 1, 1 if m == 0 else 0)
+        e_term(n, 1)
+        for way, peer in ((0, y_peers[1]), (1, y_peers[3])):
+            send(e_send.at[n, 1, rows_of(way)], e_far.at[n, way], ef_ss.at[n, way],
+                 ef_rs.at[n, way], peer)
+
+    def e_near_out(n):
+        e_term(n, 0)
+        e_near(n, 0, 1)
+        e_term(n, 2)
+        e_near(n, 1, 0)
+        e_term(n, 3)
 
     def e_near(n, way, half):
         slot, peer = (0, y_peers[1]) if way == 0 else (2, y_peers[3])
@@ -359,23 +364,19 @@
             e_p2[x] = total
 
     def e_home(k):
-        origin = xs[k]
+        origin = ys[k]
         block = e_p2.at[origin]
+
+        @pl.when(origin != x)
+        def _():
+            arrived(block, e2_rs.at[origin])
+
         if k:
-            arrived(block, e2_rs.at[origin])
-
-        @pl.when(origin == y)
-        def _():
+            send(block, e_fin.at[y], e1_ss.at[k], e1_rs.at[y], y_peers[k])
+        else:
             e_fin[y] = block[...]
 
-        @pl.when(origin != y)
-        def _():
-            pltpu.make_async_remote_copy(
-                src_ref=block, dst_ref=e_fin.at[y], send_sem=e1_ss.at[k], recv_sem=e1_rs.at[y],
-                device_id=device(x, origin, z, c), device_id_type=pl.DeviceIdType.MESH,
-            ).start()
-
-    e_out(0)
+    d_out(2)
     for k in range(1, X):
         merged_t[:, pl.ds(xs[k] * G, G)] = jnp.transpose(merged_all[xs[k]])
 
@@ -408,23 +409,28 @@
             term = merge_term(g_block(way, step), half_rows(half))
             g_out(way, step, half, term + g_in(way, step - 1, half))
 
-    d_combine()
+    e_far_out(0)
+    e_near_out(0)
+    d_out(1)
+    d_out(3)
     term = d_term(x)
     d_own[...] = term
     total = d_sums(term, x)
+    d_combine()
     for k in range(1, X):
         arrived(sx_recv.at[xs[k]], sx_rs.at[xs[k]])
         total = total + sx_recv[xs[k]]
     stats[1, t] = total
     send_stats(1)
+    g_piece(1, 1)
+    for n in (1, 2, 3):
+        e_far_out(n)
     e_combine(0)
-    e_out(1)
-    g_piece(1, 1)
-    e_out(2)
-    e_out(3)
-    e_combine(1)
+    for n in (1, 2, 3):
+        e_near_out(n)
     g_piece(2, 0)
-    e_combine(2)
+    for n in (1, 2, 3):
+        e_combine(n)
 
     means = totals(1)
     d_mean = spread(first, means)
@@ -434,7 +440,6 @@
         for half in (1 - way, way):
             arrived(d_recv_buf.at[way, rows_of(half)], d_rs.at[way, half])
         dnormed = dnormed + d_recv_buf[way].astype(F32)
-    e_combine(3)
     grad_input = (dnormed - d_mean - normed_s[0] * dn_mean) * normed_s[1]
     for q in range(4):
         part = grad_input[:, q * FS:(q + 1) * FS]
@@ -504,18 +509,16 @@
     e_sum_up(1)
     over_z(0)
     e_sum_up(2)
+    over_z(1)
     e_sum_up(3)
-    e_home(0)
-    over_z(1)
     g_piece(3, 1)
-    e_home(3)
-    e_home(2)
     back_over_z(0)
-    e_home(1)
+    for k in (1, 3, 2, 0):
+        e_home(k)
     back_over_z(1)
-    g_finish()
     back_over_x(0)
     back_over_x(1)
+    g_finish()
 
     for k in range(1, Y):
         arrived(e_fin.at[ys[k]], e1_rs.at[ys[k]])
@@ -539,14 +542,6 @@
     outputs.append(pltpu.make_async_copy(gp_ref, gp_hbm, out_s.at[2]))
     outputs[2].start()
 
-    for k in range(X):
-        @pl.when(xs[k] != y)
-        def _():
-            pltpu.make_async_remote_copy(
-                src_ref=e_p2.at[xs[k]], dst_ref=e_fin.at[y], send_sem=e1_ss.at[k],
-                recv_sem=e1_rs.at[y], device_id=device(x, xs[k], z, c),
-                device_id_type=pl.DeviceIdType.MESH,
-            ).wait_send()
     for copy in outputs:
         copy.wait()
     for copy in started:

time: 102 us -> 99.5 us (0.975)
  Pallas kernels: 100 us -> 96.6 us
    pallas_call x1, Pallas kernels: 97.7 us -> 94.3 us  [body(): pl.pallas_call(kernel, out_shape=results, in_specs=[pl.BlockSpec(memory_s...]
where the time goes in v7:
time: 99.5 us; the launch traced here: 98.1 us
  Pallas kernels  96.6 us (97%)
  between operations  1.44 us (1%)
    pallas_call x1, Pallas kernels, body(): pl.pallas_call(kernel, out_shape=results, in_specs=[pl.BlockSpec(memory_s...  94.3 us
    pallas_call x1, Pallas kernels, body(): pl.pallas_call(finish, out_shape=results, in_specs=[hbm, hbm, hbm], out_s...  2.35 us

profile of v7, /device:TPU:1, one launch (start us, length us, event | category | flops | bytes accessed | tf_op | source)
XLA Modules:
  0.0 98.1 jit_solution(11710050239648925696)
XLA Ops:
  1.3 94.3 %tower.1 = (bf16[256,1024]{1,0:T(8,128)(2,1)}, f32[640,256]{1,0:T(8,128)}, f32[160,1176]{1,0:T(8,128)}) custom-call(s32[1]{0:T(128)S(6)} %copy.8.live_ref, bf16[1176,1024]{1,0:T(8,128)(2,1)} %bitcast.5, bf16[160,1176]{1,0:T(8,128)(2,1)} %bitcast.6, bf16[640,256]{1,0:T(8,128)(2,1)} %bitcast.7, bf16[256,1024]{1,0:T(8,128)(2,1)} %emb_hbm.1), custom_call_target="tpu_custom_call" | custom-call | tf_op jit(solution)/shard_map/tower/pallas_call | solution.py:627
  95.6 2.4 %finish.1 = (bf16[256,1024]{1,0:T(8,128)(2,1)}, f32[640,256]{1,0:T(8,128)}, f32[160,1176]{1,0:T(8,128)}) custom-call(bf16[256,1024]{1,0:T(8,128)(2,1)} %get-tuple-element.9.embeds_in, f32[640,256]{1,0:T(8,128)} %get-tuple-element.10.gm_in, f32[160,1176]{1,0:T(8,128)} %get-tuple-element.11.gp_in), custom_call_target="tpu_custom_call" | custom-call | tf_op jit(solution)/shard_map/finish/pallas_call | solution.py:638

commit v8 on v7

--- a/solution.py
+++ b/solution.py
@@ -429,7 +429,7 @@
     for n in (1, 2, 3):
         e_near_out(n)
     g_piece(2, 0)
-    for n in (1, 2, 3):
+    for n in (1, 2):
         e_combine(n)
 
     means = totals(1)
@@ -450,6 +450,8 @@
     grad_rows = jnp.concatenate([proj_s[0], proj_s[1]], axis=1)
     grad_rows = jnp.transpose(grad_rows)[:FS].astype(BF16)
 
+    e_combine(3)
+
     for chunk in (0, 1):
         low, high = 640 * chunk, min(640 * (chunk + 1), PD)
         if chunk:
@@ -511,11 +513,11 @@
     e_sum_up(2)
     over_z(1)
     e_sum_up(3)
-    g_piece(3, 1)
     back_over_z(0)
     for k in (1, 3, 2, 0):
         e_home(k)
     back_over_z(1)
+    g_piece(3, 1)
     back_over_x(0)
     back_over_x(1)
     g_finish()

time: 99.5 us -> 98.2 us (0.987); the launches traced: 98.1 us -> 98.1 us
  no operation moved by 1% of the time
where the time goes in v8:
time: 98.2 us; the launch traced here: 98.1 us
  Pallas kernels  96.6 us (98%)
  between operations  1.44 us (1%)
    pallas_call x1, Pallas kernels, body(): pl.pallas_call(kernel, out_shape=results, in_specs=[pl.BlockSpec(memory_s...  94.3 us
    pallas_call x1, Pallas kernels, body(): pl.pallas_call(finish, out_shape=results, in_specs=[hbm, hbm, hbm], out_s...  2.35 us

profile of v8, /device:TPU:1, one launch (start us, length us, event | category | flops | bytes accessed | tf_op | source)
XLA Modules:
  0.0 98.1 jit_solution(5369979090892574641)
XLA Ops:
  1.3 94.3 %tower.1 = (bf16[256,1024]{1,0:T(8,128)(2,1)}, f32[640,256]{1,0:T(8,128)}, f32[160,1176]{1,0:T(8,128)}) custom-call(s32[1]{0:T(128)S(6)} %copy.8.live_ref, bf16[1176,1024]{1,0:T(8,128)(2,1)} %bitcast.5, bf16[160,1176]{1,0:T(8,128)(2,1)} %bitcast.6, bf16[640,256]{1,0:T(8,128)(2,1)} %bitcast.7, bf16[256,1024]{1,0:T(8,128)(2,1)} %emb_hbm.1), custom_call_target="tpu_custom_call" | custom-call | tf_op jit(solution)/shard_map/tower/pallas_call | solution.py:629
  95.5 2.4 %finish.1 = (bf16[256,1024]{1,0:T(8,128)(2,1)}, f32[640,256]{1,0:T(8,128)}, f32[160,1176]{1,0:T(8,128)}) custom-call(bf16[256,1024]{1,0:T(8,128)(2,1)} %get-tuple-element.9.embeds_in, f32[640,256]{1,0:T(8,128)} %get-tuple-element.10.gm_in, f32[160,1176]{1,0:T(8,128)} %get-tuple-element.11.gp_in), custom_call_target="tpu_custom_call" | custom-call | tf_op jit(solution)/shard_map/finish/pallas_call | solution.py:640
